TPU v7x, 32 devices: a whole 2x2x4 slice. The times are simulated.
32 devices in a mesh: rows: 4 (over x, core), mp: 8 (over z, y).
Axes of the slice: x: 2, y: 2, z: 4, core: 2. Of those that a mesh axis runs over, the one named last changes fastest.
Arguments:
- inputs: bfloat16 [3, 512, 2304], P(None, 'rows', 'mp'), may hold values from -6 to 6
- gate_up: bfloat16 [3, 2304, 2, 9216], P(None, None, None, 'mp'), may hold values from -0.125 to 0.125
- down_weight: bfloat16 [3, 9216, 2304], P(None, 'mp'), may hold values from -0.09375 to 0.09375
- enc_weight: bfloat16 [3, 2304, 16384], P(None, None, 'mp'), may hold values from -0.125 to 0.125
- enc_bias: float32 [3, 16384], P(None, 'mp'), may hold values from -3 to 3
- dec_weight: bfloat16 [6, 16384, 2304], P(None, 'mp', 'rows'), may hold values from -0.09375 to 0.09375
Outputs:
- recon: float32 [3, 512, 2304], P(None, 'rows', 'mp')
- residual: float32 [3, 512, 2304], P(None, 'rows', 'mp')
All inputs are finite; a program needn't handle non-finite values.
Results may differ from a plain program's by a relative error of at most 0.0029.
Values may be sent and summed in bfloat16 or wider, within the bound.
A program may use at most 256 MiB of HBM per device.

v0:
```python
import functools

import jax
import jax.numpy as jnp
from jax import lax
from jax.experimental import pallas as pl
from jax.experimental.pallas import tpu as pltpu
from jax.sharding import PartitionSpec as P


def flip_permutation(count):
    return [(index, index ^ 1) for index in range(count)]


def shift_permutation(count, inner, distance):
    outer = count // inner
    return [
        (index, ((index // inner + distance) % outer) * inner + index % inner)
        for index in range(count)
    ]


def gather_inputs(rows_in, me, count):
    outer = count // 2
    position, parity = me // 2, me % 2
    parts = [rows_in] + [
        lax.ppermute(rows_in, "mp", shift_permutation(count, 2, distance))
        for distance in range(1, outer)
    ]
    around = jnp.stack([parts[(-index) % outer] for index in range(2 * outer - 1)])
    mine = lax.dynamic_slice_in_dim(around, (outer - position) % outer, outer, 0)
    other = lax.ppermute(mine, "mp", flip_permutation(count))
    even = jnp.where(parity == 0, mine, other)
    odd = jnp.where(parity == 0, other, mine)
    both = jnp.stack([even, odd], axis=1)
    rows, width = rows_in.shape
    return both.transpose(2, 0, 1, 3).reshape(rows, count * width)


def gather_rows(latent, me, count):
    outer = count // 2
    position, parity = me // 2, me % 2
    parts = [latent] + [
        lax.ppermute(latent, "rows", shift_permutation(count, 2, distance))
        for distance in range(1, outer)
    ]
    around = jnp.stack([parts[(-index) % outer] for index in range(2 * outer - 1)])
    mine = lax.dynamic_slice_in_dim(around, (outer - position) % outer, outer, 0)
    other = lax.ppermute(mine, "rows", flip_permutation(count))
    even = jnp.where(parity == 0, mine, other)
    odd = jnp.where(parity == 0, other, mine)
    both = jnp.stack([even, odd], axis=1)
    return both.reshape(count * latent.shape[0], latent.shape[1])


def scatter_sum(pieces, me, count):
    outer = count // 2
    position, parity = me // 2, me % 2
    split = pieces.reshape((outer, 2) + pieces.shape[1:])
    sent = jnp.where(parity == 0, split[:, 1], split[:, 0]).astype(jnp.bfloat16)
    kept = jnp.where(parity == 0, split[:, 0], split[:, 1])
    arrived = lax.ppermute(sent, "mp", flip_permutation(count))
    summed = kept + arrived.astype(jnp.float32)
    total = lax.dynamic_index_in_dim(summed, position, 0, keepdims=False)
    narrow = summed.astype(jnp.bfloat16)
    for distance in range(1, outer):
        block = lax.dynamic_index_in_dim(
            narrow, (position + distance) % outer, 0, keepdims=False
        )
        arrived = lax.ppermute(block, "mp", shift_permutation(count, 2, distance))
        total = total + arrived.astype(jnp.float32)
    return total


def hidden_kernel(spread_ref, weight_ref, hidden_ref, total_ref):
    step = pl.program_id(0)
    depth, _, columns = weight_ref.shape[1:]

    @pl.when(step == 0)
    def _():
        total_ref[...] = jnp.zeros_like(total_ref)

    weight = weight_ref[0].reshape(2 * depth, columns)
    total_ref[...] += jnp.dot(spread_ref[...], weight, preferred_element_type=jnp.float32)

    @pl.when(step == pl.num_programs(0) - 1)
    def _():
        rows = hidden_ref.shape[0]
        gate, upper = total_ref[:rows], total_ref[rows:]
        hidden = jax.nn.gelu(gate, approximate=True) * upper
        hidden_ref[...] = hidden.astype(hidden_ref.dtype)


def hidden_units(rows_in, gate_up, layer):
    rows, model_width = rows_in.shape
    hidden_local = gate_up.shape[3]
    depth = max(d for d in range(128, 385, 128) if model_width % d == 0)
    zeros = jnp.zeros_like(rows_in)
    spread = jnp.concatenate(
        [jnp.stack([rows_in, zeros], axis=2), jnp.stack([zeros, rows_in], axis=2)]
    ).reshape(2 * rows, 2 * model_width)
    return pl.pallas_call(
        hidden_kernel,
        grid=(model_width // depth,),
        in_specs=[
            pl.BlockSpec((2 * rows, 2 * depth), lambda step: (0, step)),
            pl.BlockSpec((1, depth, 2, hidden_local), lambda step: (layer, step, 0, 0)),
        ],
        out_specs=pl.BlockSpec((rows, hidden_local), lambda step: (0, 0)),
        out_shape=jax.ShapeDtypeStruct((rows, hidden_local), jnp.bfloat16),
        scratch_shapes=[pltpu.VMEM((2 * rows, hidden_local), jnp.float32)],
        cost_estimate=pl.CostEstimate(
            flops=8 * rows * model_width * hidden_local,
            bytes_accessed=4 * model_width * hidden_local,
            transcendentals=rows * hidden_local,
        ),
        compiler_params=pltpu.CompilerParams(vmem_limit_bytes=24 * 1024 * 1024),
    )(spread, gate_up)


def body(inputs, gate_up, down_weight, enc_weight, enc_bias, dec_weight):
    layers, rows, width = inputs.shape
    across, count = lax.axis_size("rows"), lax.axis_size("mp")
    my_row, me = lax.axis_index("rows"), lax.axis_index("mp")
    blocks = count // across

    gathered = [gather_inputs(inputs[layer], me, count) for layer in range(layers)]
    latents = []
    for layer in range(layers):
        pre = jnp.dot(gathered[layer], enc_weight[layer], preferred_element_type=jnp.float32)
        latent = jax.nn.relu(pre + enc_bias[layer][None, :]).astype(jnp.bfloat16)
        latents.append(gather_rows(latent, my_row, across))
    targets = []
    for layer in range(layers):
        hidden = hidden_units(gathered[layer], gate_up, layer)
        partial = jnp.dot(hidden, down_weight[layer], preferred_element_type=jnp.float32)
        partial = lax.optimization_barrier(partial)
        pieces = partial.reshape(rows, count, width).transpose(1, 0, 2)
        targets.append(scatter_sum(pieces, me, count))
    home = [
        (r * count + a * blocks + c, a * count + r * blocks + c)
        for r in range(across)
        for a in range(across)
        for c in range(blocks)
    ]
    recons = []
    for target in range(layers):
        partial = sum(
            jnp.dot(
                latents[source],
                dec_weight[target * (target + 1) // 2 + source],
                preferred_element_type=jnp.float32,
            )
            for source in range(target + 1)
        )
        pieces = partial.reshape(across, rows, blocks, width).transpose(0, 2, 1, 3)
        summed = scatter_sum(pieces.reshape(count, rows, width), me, count)
        recons.append(lax.ppermute(summed, ("rows", "mp"), home))
    recon = jnp.stack(recons)
    residual = jnp.stack(targets) - recon
    return (recon, residual)


def solution(mesh):
    in_specs = (
        P(None, "rows", "mp"),
        P(None, None, None, "mp"),
        P(None, "mp", None),
        P(None, None, "mp"),
        P(None, "mp"),
        P(None, "mp", "rows"),
    )
    out_specs = (P(None, "rows", "mp"), P(None, "rows", "mp"))
    return jax.shard_map(body, mesh=mesh, in_specs=in_specs, out_specs=out_specs, check_vma=False)
```

profile of v0, /device:TPU:2, one launch (start us, length us, event | category | flops | bytes accessed | tf_op | source)
XLA Modules:
  0.0 261.1 jit_solution(13357235970368663055)
XLA Ops:
  1.7 3.7 %collective-permute-start = (bf16[128,288]{0,1:T(8,128)(2,1)S(1)}, bf16[128,288]{0,1:T(8,128)(2,1)S(1)}, u32[]{:S(2)}, u32[]{:S(2)}) collective-permute-start(bf16[128,288]{0,1:T(8,128)(2,1)S(1)} %get-tuple-element.49), channel_id=1, source_target_pairs={{0,6},{1,7},{2,0},{3,1},{4,2},{5,3},{6,4},{7,5},{8,14},{9,15},{10,... | collective-permute-start | bytes 221192 | tf_op jit(solution)/shard_map/ppermute | solution.py:27
  15.7 3.2 %collective-permute-start.23 = (bf16[128,288]{0,1:T(8,128)(2,1)S(1)}, bf16[128,288]{0,1:T(8,128)(2,1)S(1)}, u32[]{:S(2)}, u32[]{:S(2)}) collective-permute-start(bf16[128,288]{0,1:T(8,128)(2,1)S(1)} %get-tuple-element.53), channel_id=1, source_target_pairs={{0,4},{1,5},{2,6},{3,7},{4,0},{5,1},{6,2},{7,3},{8,12},{9,13},{10,... | collective-permute-start | bytes 221192 | tf_op jit(solution)/shard_map/ppermute | solution.py:27
  29.8 5.5 %collective-permute-done.25 = bf16[4,128,288]{1,2,0:T(8,128)(2,1)S(1)} collective-permute-done((bf16[4,128,288]{1,2,0:T(8,128)(2,1)S(1)}, bf16[4,128,288]{1,2,0:T(8,128)(2,1)S(1)}, u32[]{:S(2)}, u32[]{:S(2)}) %collective-permute-start.25) | collective-permute-done | bytes 294944 | tf_op jit(solution)/shard_map/ppermute | solution.py:32
  36.5 14.4 %copy.37 = bf16[256,2304,2]{0,2,1:T(2,128)(2,1)S(1)} copy(bf16[256,2304,2]{0,1,2:T(8,128)(2,1)S(1)} %fusion.53) | data formatting | bytes 4718592 | tf_op jit(solution)/shard_map/concatenate | solution.py:99
  56.1 8.0 %shard_map.79 = bf16[128,1152]{1,0:T(8,128)(2,1)S(1)} custom-call(bf16[256,4608]{1,0:T(8,128)(2,1)S(1)} %copy.38.spread_ref, bf16[3,2304,2,1152]{3,2,1,0:T(2,128)(2,1)} %weight_ref.5), custom_call_target="tpu_custom_call" | custom-call | flops 2717908992 | bytes 10616832 | tf_op jit(solution)/shard_map/pallas_call | solution.py:102
  64.1 3.4 %fusion.9 = f32[128,2304]{1,0:T(8,128)S(1)} fusion(bf16[128,1152]{1,0:T(8,128)(2,1)S(1)} %shard_map.79, bf16[3,1152,2304]{2,1,0:T(8,128)(2,1)} %param.8), kind=kOutput, calls=%fused_computation.9 | convolution fusion | flops 679477248 | bytes 6782976 | tf_op jit(solution)/shard_map/dot_general | solution.py:136
  71.5 14.4 %copy.31 = bf16[256,2304,2]{0,2,1:T(2,128)(2,1)S(1)} copy(bf16[256,2304,2]{0,1,2:T(8,128)(2,1)S(1)} %fusion.52) | data formatting | bytes 4718592 | tf_op jit(solution)/shard_map/concatenate | solution.py:99
  91.0 8.0 %shard_map.78 = bf16[128,1152]{1,0:T(8,128)(2,1)S(1)} custom-call(bf16[256,4608]{1,0:T(8,128)(2,1)S(1)} %copy.32.spread_ref, bf16[3,2304,2,1152]{3,2,1,0:T(2,128)(2,1)} %weight_ref.5), custom_call_target="tpu_custom_call" | custom-call | flops 2717908992 | bytes 10616832 | tf_op jit(solution)/shard_map/pallas_call | solution.py:102
  99.0 3.5 %fusion.11 = f32[128,2304]{1,0:T(8,128)S(1)} fusion(bf16[128,1152]{1,0:T(8,128)(2,1)S(1)} %shard_map.78, bf16[3,1152,2304]{2,1,0:T(8,128)(2,1)} %param.8), kind=kOutput, calls=%fused_computation.11 | convolution fusion | flops 679477248 | bytes 6782976 | tf_op jit(solution)/shard_map/dot_general | solution.py:136
  106.2 14.3 %copy.25 = bf16[256,2304,2]{0,2,1:T(2,128)(2,1)S(1)} copy(bf16[256,2304,2]{0,1,2:T(8,128)(2,1)S(1)} %fusion.51) | data formatting | bytes 4718592 | tf_op jit(solution)/shard_map/concatenate | solution.py:99
  125.7 8.2 %shard_map.77 = bf16[128,1152]{1,0:T(8,128)(2,1)S(1)} custom-call(bf16[256,4608]{1,0:T(8,128)(2,1)S(1)} %copy.26.spread_ref, bf16[3,2304,2,1152]{3,2,1,0:T(2,128)(2,1)} %weight_ref.5), custom_call_target="tpu_custom_call" | custom-call | flops 2717908992 | bytes 10616832 | tf_op jit(solution)/shard_map/pallas_call | solution.py:102
  133.9 4.5 %fusion.13 = f32[128,2304]{1,0:T(8,128)} fusion(bf16[128,1152]{1,0:T(8,128)(2,1)S(1)} %shard_map.77, bf16[3,1152,2304]{2,1,0:T(8,128)(2,1)} %param.8), kind=kOutput, calls=%fused_computation.13 | convolution fusion | flops 679477248 | bytes 6782976 | tf_op jit(solution)/shard_map/dot_general | solution.py:136
  141.7 5.2 %fusion.42 = bf16[128,2048]{1,0:T(8,128)(2,1)S(1)} fusion(bf16[128,2304]{0,1:T(8,128)(2,1)S(1)} %bitcast.399, bf16[3,2304,2048]{2,1,0:T(8,128)(2,1)} %param.9, f32[2048]{0:T(1024)S(1)} %bitcast.427), kind=kOutput, calls=%fused_computation.32 | convolution fusion | flops 1208745984 | bytes 10559488 | tf_op jit(solution)/shard_map/dot_general | solution.py:130
  147.5 5.2 %fusion.45 = bf16[128,2048]{1,0:T(8,128)(2,1)S(1)} fusion(bf16[128,2304]{0,1:T(8,128)(2,1)S(1)} %bitcast.401, bf16[3,2304,2048]{2,1,0:T(8,128)(2,1)} %param.9, f32[2048]{0:T(1024)S(1)} %bitcast.426), kind=kOutput, calls=%fused_computation.33 | convolution fusion | flops 1208745984 | bytes 10559488 | tf_op jit(solution)/shard_map/dot_general | solution.py:130
  154.2 5.3 %fusion.48 = bf16[128,2048]{1,0:T(8,128)(2,1)S(1)} fusion(bf16[128,2304]{0,1:T(8,128)(2,1)S(1)} %bitcast.403, bf16[3,2304,2048]{2,1,0:T(8,128)(2,1)} %param.9, f32[2048]{0:T(1024)S(1)} %bitcast.425), kind=kOutput, calls=%fused_computation.34 | convolution fusion | flops 1208745984 | bytes 10559488 | tf_op jit(solution)/shard_map/dot_general | solution.py:130
  174.3 4.9 %collective-permute-done.39 = bf16[128,288]{0,1:T(8,128)(2,1)S(1)} collective-permute-done((bf16[128,288]{0,1:T(8,128)(2,1)S(1)}, bf16[128,288]{0,1:T(8,128)(2,1)S(1)}, u32[]{:S(2)}, u32[]{:S(2)}) %collective-permute-start.39) | collective-permute-done | bytes 73760 | tf_op jit(solution)/shard_map/ppermute | solution.py:70
  199.4 3.4 %fusion.69 = f32[512,576]{0,1:T(8,128)S(1)} fusion(f32[512,576]{0,1:T(8,128)} %fusion.60, bf16[512,2048]{1,0:T(8,128)(2,1)S(1)} %bitcast.418, bf16[6,2048,576]{1,2,0:T(8,128)(2,1)} %param.11), kind=kOutput, calls=%fused_computation.66 | convolution fusion | flops 1208254464 | bytes 6815744 | tf_op jit(solution)/shard_map/dot_general | solution.py:149
  216.4 3.8 %collective-permute-done.6 = bf16[4,128,288]{1,2,0:T(8,128)(2,1)S(1)} collective-permute-done((bf16[4,128,288]{1,2,0:T(8,128)(2,1)S(1)}, bf16[4,128,288]{1,2,0:T(8,128)(2,1)S(1)}, u32[]{:S(2)}, u32[]{:S(2)}) %collective-permute-start.6) | collective-permute-done | bytes 294944 | tf_op jit(solution)/shard_map/ppermute | solution.py:62
  221.2 3.0 %collective-permute-start.20 = (bf16[128,288]{0,1:T(8,128)(2,1)S(1)}, bf16[128,288]{0,1:T(8,128)(2,1)S(1)}, u32[]{:S(2)}, u32[]{:S(2)}) collective-permute-start(bf16[128,288]{0,1:T(8,128)(2,1)S(1)} %get-tuple-element.32), channel_id=1, source_target_pairs={{0,6},{1,7},{2,0},{3,1},{4,2},{5,3},{6,4},{7,5},{8,14},{9,15},{10,... | collective-permute-start | bytes 221192 | tf_op jit(solution)/shard_map/ppermute | solution.py:70
  226.8 3.9 %collective-permute-start.9 = (bf16[128,288]{0,1:T(8,128)(2,1)S(1)}, bf16[128,288]{0,1:T(8,128)(2,1)S(1)}, u32[]{:S(2)}, u32[]{:S(2)}) collective-permute-start(bf16[128,288]{0,1:T(8,128)(2,1)S(1)} %get-tuple-element.29), channel_id=1, source_target_pairs={{0,6},{1,7},{2,0},{3,1},{4,2},{5,3},{6,4},{7,5},{8,14},{9,15},{10,... | collective-permute-start | bytes 221192 | tf_op jit(solution)/shard_map/ppermute | solution.py:70
  233.6 4.0 %collective-permute-start.34 = (bf16[128,288]{0,1:T(8,128)(2,1)S(1)}, bf16[128,288]{0,1:T(8,128)(2,1)S(1)}, u32[]{:S(2)}, u32[]{:S(2)}) collective-permute-start(bf16[128,288]{0,1:T(8,128)(2,1)S(1)} %copy-done.14), channel_id=1, source_target_pairs={{0,2},{1,3},{2,4},{3,5},{4,6},{5,7},{6,0},{7,1},{8,10},{9,11},{10,... | collective-permute-start | bytes 221192 | tf_op jit(solution)/shard_map/ppermute | solution.py:70
  240.4 5.3 %collective-permute-start.21 = (f32[128,288]{0,1:T(8,128)S(1)}, f32[128,288]{0,1:T(8,128)S(1)}, u32[]{:S(2)}, u32[]{:S(2)}) collective-permute-start(f32[128,288]{0,1:T(8,128)S(1)} %fusion.104), channel_id=1, source_target_pairs={{0,0},{1,1},{2,8},{3,9},{4,16},{5,17},{6,24},{7,25},{8,2},{9,3},{1... | collective-permute-start | bytes 442376 | tf_op jit(solution)/shard_map/ppermute | solution.py:158
  249.2 4.1 %collective-permute-done.32 = f32[128,288]{0,1:T(8,128)S(1)} collective-permute-done((f32[128,288]{0,1:T(8,128)S(1)}, f32[128,288]{0,1:T(8,128)S(1)}, u32[]{:S(2)}, u32[]{:S(2)}) %collective-permute-start.32) | collective-permute-done | bytes 147488 | tf_op jit(solution)/shard_map/ppermute | solution.py:158
  253.2 4.7 %collective-permute-done.21 = f32[128,288]{0,1:T(8,128)S(1)} collective-permute-done((f32[128,288]{0,1:T(8,128)S(1)}, f32[128,288]{0,1:T(8,128)S(1)}, u32[]{:S(2)}, u32[]{:S(2)}) %collective-permute-start.21) | collective-permute-done | bytes 147488 | tf_op jit(solution)/shard_map/ppermute | solution.py:158
  (208 shorter events, 116.0 us)
Async XLA Ops:
  1.7 10.1 %collective-permute-start = (bf16[128,288]{0,1:T(8,128)(2,1)S(1)}, bf16[128,288]{0,1:T(8,128)(2,1)S(1)}, u32[]{:S(2)}, u32[]{:S(2)}) collective-permute-start(bf16[128,288]{0,1:T(8,128)(2,1)S(1)} %get-tuple-element.49), channel_id=1, source_target_pairs={{0,6},{1,7},{2,0},{3,1},{4,2},{5,3},{6,4},{7,5},{8,14},{9,15},{10,... | collective-permute-start | bytes 221192 | tf_op jit(solution)/shard_map/ppermute | solution.py:27
  5.3 10.4 %collective-permute-start.2 = (bf16[128,288]{0,1:T(8,128)(2,1)S(1)}, bf16[128,288]{0,1:T(8,128)(2,1)S(1)}, u32[]{:S(2)}, u32[]{:S(2)}) collective-permute-start(bf16[128,288]{0,1:T(8,128)(2,1)S(1)} %get-tuple-element.49), channel_id=1, source_target_pairs={{0,2},{1,3},{2,4},{3,5},{4,6},{5,7},{6,0},{7,1},{8,10},{9,11},{10,... | collective-permute-start | bytes 221192 | tf_op jit(solution)/shard_map/ppermute | solution.py:27
  6.3 12.6 %collective-permute-start.11 = (bf16[128,288]{0,1:T(8,128)(2,1)S(1)}, bf16[128,288]{0,1:T(8,128)(2,1)S(1)}, u32[]{:S(2)}, u32[]{:S(2)}) collective-permute-start(bf16[128,288]{0,1:T(8,128)(2,1)S(1)} %get-tuple-element.54), channel_id=1, source_target_pairs={{0,6},{1,7},{2,0},{3,1},{4,2},{5,3},{6,4},{7,5},{8,14},{9,15},{10,... | collective-permute-start | bytes 221192 | tf_op jit(solution)/shard_map/ppermute | solution.py:27
  9.1 12.1 %collective-permute-start.12 = (bf16[128,288]{0,1:T(8,128)(2,1)S(1)}, bf16[128,288]{0,1:T(8,128)(2,1)S(1)}, u32[]{:S(2)}, u32[]{:S(2)}) collective-permute-start(bf16[128,288]{0,1:T(8,128)(2,1)S(1)} %get-tuple-element.54), channel_id=1, source_target_pairs={{0,4},{1,5},{2,6},{3,7},{4,0},{5,1},{6,2},{7,3},{8,12},{9,13},{10,... | collective-permute-start | bytes 221192 | tf_op jit(solution)/shard_map/ppermute | solution.py:27
  25.3 10.0 %collective-permute-start.25 = (bf16[4,128,288]{1,2,0:T(8,128)(2,1)S(1)}, bf16[4,128,288]{1,2,0:T(8,128)(2,1)S(1)}, u32[]{:S(2)}, u32[]{:S(2)}) collective-permute-start(bf16[4,128,288]{1,2,0:T(8,128)(2,1)S(1)} %constant_dynamic-slice_fusion), channel_id=1, source_target_pairs={{0,1},{1,0},{2,3},{3,2},{4,5},{5,4},{6,7},{7,6},{8,9},{9,8},{10,11... | collective-permute-start | bytes 884744 | tf_op jit(solution)/shard_map/ppermute | solution.py:32
  26.9 43.3 %collective-permute-start.14 = (bf16[4,128,288]{1,2,0:T(8,128)(2,1)S(1)}, bf16[4,128,288]{1,2,0:T(8,128)(2,1)S(1)}, u32[]{:S(2)}, u32[]{:S(2)}) collective-permute-start(bf16[4,128,288]{1,2,0:T(8,128)(2,1)S(1)} %constant_dynamic-slice_fusion.1), channel_id=1, source_target_pairs={{0,1},{1,0},{2,3},{3,2},{4,5},{5,4},{6,7},{7,6},{8,9},{9,8},{10,11... | collective-permute-start | bytes 884744 | tf_op jit(solution)/shard_map/ppermute | solution.py:32
  28.3 75.9 %collective-permute-start.3 = (bf16[4,128,288]{1,2,0:T(8,128)(2,1)}, bf16[4,128,288]{1,2,0:T(8,128)(2,1)}, u32[]{:S(2)}, u32[]{:S(2)}) collective-permute-start(bf16[4,128,288]{1,2,0:T(8,128)(2,1)} %constant_dynamic-slice_fusion.2), channel_id=1, source_target_pairs={{0,1},{1,0},{2,3},{3,2},{4,5},{5,4},{6,7},{7,6},{8,9},{9,8},{10,11... | collective-permute-start | bytes 884744 | tf_op jit(solution)/shard_map/ppermute | solution.py:32
  68.7 90.8 %collective-permute-start.41 = (bf16[4,128,288]{1,2,0:T(8,128)(2,1)}, bf16[4,128,288]{1,2,0:T(8,128)(2,1)}, u32[]{:S(2)}, u32[]{:S(2)}) collective-permute-start(bf16[4,128,288]{1,2,0:T(8,128)(2,1)} %fusion.91), channel_id=1, source_target_pairs={{0,1},{1,0},{2,3},{3,2},{4,5},{5,4},{6,7},{7,6},{8,9},{9,8},{10,11... | collective-permute-start | bytes 884744 | tf_op jit(solution)/shard_map/ppermute | solution.py:62
  103.7 58.9 %collective-permute-start.37 = (bf16[4,128,288]{1,2,0:T(8,128)(2,1)}, bf16[4,128,288]{1,2,0:T(8,128)(2,1)}, u32[]{:S(2)}, u32[]{:S(2)}) collective-permute-start(bf16[4,128,288]{1,2,0:T(8,128)(2,1)} %fusion.90), channel_id=1, source_target_pairs={{0,1},{1,0},{2,3},{3,2},{4,5},{5,4},{6,7},{7,6},{8,9},{9,8},{10,11... | collective-permute-start | bytes 884744 | tf_op jit(solution)/shard_map/ppermute | solution.py:62
  140.1 23.6 %collective-permute-start.33 = (bf16[4,128,288]{1,2,0:T(8,128)(2,1)S(1)}, bf16[4,128,288]{1,2,0:T(8,128)(2,1)S(1)}, u32[]{:S(2)}, u32[]{:S(2)}) collective-permute-start(bf16[4,128,288]{1,2,0:T(8,128)(2,1)S(1)} %fusion.89), channel_id=1, source_target_pairs={{0,1},{1,0},{2,3},{3,2},{4,5},{5,4},{6,7},{7,6},{8,9},{9,8},{10,11... | collective-permute-start | bytes 884744 | tf_op jit(solution)/shard_map/ppermute | solution.py:62
  146.9 33.8 %collective-permute-start.26 = (bf16[128,2048]{1,0:T(8,128)(2,1)S(1)}, bf16[128,2048]{1,0:T(8,128)(2,1)S(1)}, u32[]{:S(2)}, u32[]{:S(2)}) collective-permute-start(bf16[128,2048]{1,0:T(8,128)(2,1)S(1)} %fusion.42), channel_id=1, source_target_pairs={{0,16},{8,24},{16,0},{24,8},{1,17},{9,25},{17,1},{25,9},{2,18},{10... | collective-permute-start | bytes 1572872 | tf_op jit(solution)/shard_map/ppermute | solution.py:44
  152.7 14.7 %collective-permute-start.15 = (bf16[128,2048]{1,0:T(8,128)(2,1)S(1)}, bf16[128,2048]{1,0:T(8,128)(2,1)S(1)}, u32[]{:S(2)}, u32[]{:S(2)}) collective-permute-start(bf16[128,2048]{1,0:T(8,128)(2,1)S(1)} %fusion.45), channel_id=1, source_target_pairs={{0,16},{8,24},{16,0},{24,8},{1,17},{9,25},{17,1},{25,9},{2,18},{10... | collective-permute-start | bytes 1572872 | tf_op jit(solution)/shard_map/ppermute | solution.py:44
  169.1 15.8 %collective-permute-start.16 = (bf16[2,128,2048]{2,1,0:T(8,128)(2,1)S(1)}, bf16[2,128,2048]{2,1,0:T(8,128)(2,1)S(1)}, u32[]{:S(2)}, u32[]{:S(2)}) collective-permute-start(bf16[2,128,2048]{2,1,0:T(8,128)(2,1)S(1)} %fusion.81), channel_id=1, source_target_pairs={{0,8},{8,0},{16,24},{24,16},{1,9},{9,1},{17,25},{25,17},{2,10},{10... | collective-permute-start | bytes 3145736 | tf_op jit(solution)/shard_map/ppermute | solution.py:49
  169.9 14.3 %collective-permute-start.4 = (bf16[128,2048]{1,0:T(8,128)(2,1)S(1)}, bf16[128,2048]{1,0:T(8,128)(2,1)S(1)}, u32[]{:S(2)}, u32[]{:S(2)}) collective-permute-start(bf16[128,2048]{1,0:T(8,128)(2,1)S(1)} %fusion.48), channel_id=1, source_target_pairs={{0,16},{8,24},{16,0},{24,8},{1,17},{9,25},{17,1},{25,9},{2,18},{10... | collective-permute-start | bytes 1572872 | tf_op jit(solution)/shard_map/ppermute | solution.py:44
  179.2 66.5 %collective-permute-start.36 = (bf16[128,288]{0,1:T(8,128)(2,1)}, bf16[128,288]{0,1:T(8,128)(2,1)}, u32[]{:S(2)}, u32[]{:S(2)}) collective-permute-start(bf16[128,288]{0,1:T(8,128)(2,1)} %get-tuple-element.38), channel_id=1, source_target_pairs={{0,6},{1,7},{2,0},{3,1},{4,2},{5,3},{6,4},{7,5},{8,14},{9,15},{10,... | collective-permute-start | bytes 221192 | tf_op jit(solution)/shard_map/ppermute | solution.py:70
  179.5 68.7 %collective-permute-start.35 = (bf16[128,288]{0,1:T(8,128)(2,1)}, bf16[128,288]{0,1:T(8,128)(2,1)}, u32[]{:S(2)}, u32[]{:S(2)}) collective-permute-start(bf16[128,288]{0,1:T(8,128)(2,1)} %get-tuple-element.39), channel_id=1, source_target_pairs={{0,4},{1,5},{2,6},{3,7},{4,0},{5,1},{6,2},{7,3},{8,12},{9,13},{10,... | collective-permute-start | bytes 221192 | tf_op jit(solution)/shard_map/ppermute | solution.py:70
  198.6 10.7 %collective-permute-start.28 = (bf16[4,128,288]{1,2,0:T(8,128)(2,1)}, bf16[4,128,288]{1,2,0:T(8,128)(2,1)}, u32[]{:S(2)}, u32[]{:S(2)}) collective-permute-start(bf16[4,128,288]{1,2,0:T(8,128)(2,1)} %fusion.88), channel_id=1, source_target_pairs={{0,1},{1,0},{2,3},{3,2},{4,5},{5,4},{6,7},{7,6},{8,9},{9,8},{10,11... | collective-permute-start | bytes 884744 | tf_op jit(solution)/shard_map/ppermute | solution.py:62
  203.7 11.3 %collective-permute-start.17 = (bf16[4,128,288]{1,2,0:T(8,128)(2,1)S(1)}, bf16[4,128,288]{1,2,0:T(8,128)(2,1)S(1)}, u32[]{:S(2)}, u32[]{:S(2)}) collective-permute-start(bf16[4,128,288]{1,2,0:T(8,128)(2,1)S(1)} %fusion.87), channel_id=1, source_target_pairs={{0,1},{1,0},{2,3},{3,2},{4,5},{5,4},{6,7},{7,6},{8,9},{9,8},{10,11... | collective-permute-start | bytes 884744 | tf_op jit(solution)/shard_map/ppermute | solution.py:62
  208.0 12.1 %collective-permute-start.6 = (bf16[4,128,288]{1,2,0:T(8,128)(2,1)S(1)}, bf16[4,128,288]{1,2,0:T(8,128)(2,1)S(1)}, u32[]{:S(2)}, u32[]{:S(2)}) collective-permute-start(bf16[4,128,288]{1,2,0:T(8,128)(2,1)S(1)} %fusion.86), channel_id=1, source_target_pairs={{0,1},{1,0},{2,3},{3,2},{4,5},{5,4},{6,7},{7,6},{8,9},{9,8},{10,11... | collective-permute-start | bytes 884744 | tf_op jit(solution)/shard_map/ppermute | solution.py:62
  210.3 10.8 %collective-permute-start.31 = (bf16[128,288]{0,1:T(8,128)(2,1)S(1)}, bf16[128,288]{0,1:T(8,128)(2,1)S(1)}, u32[]{:S(2)}, u32[]{:S(2)}) collective-permute-start(bf16[128,288]{0,1:T(8,128)(2,1)S(1)} %get-tuple-element.35), channel_id=1, source_target_pairs={{0,6},{1,7},{2,0},{3,1},{4,2},{5,3},{6,4},{7,5},{8,14},{9,15},{10,... | collective-permute-start | bytes 221192 | tf_op jit(solution)/shard_map/ppermute | solution.py:70
  233.6 14.6 %collective-permute-start.34 = (bf16[128,288]{0,1:T(8,128)(2,1)S(1)}, bf16[128,288]{0,1:T(8,128)(2,1)S(1)}, u32[]{:S(2)}, u32[]{:S(2)}) collective-permute-start(bf16[128,288]{0,1:T(8,128)(2,1)S(1)} %copy-done.14), channel_id=1, source_target_pairs={{0,2},{1,3},{2,4},{3,5},{4,6},{5,7},{6,0},{7,1},{8,10},{9,11},{10,... | collective-permute-start | bytes 221192 | tf_op jit(solution)/shard_map/ppermute | solution.py:70
  238.0 15.2 %collective-permute-start.32 = (f32[128,288]{0,1:T(8,128)S(1)}, f32[128,288]{0,1:T(8,128)S(1)}, u32[]{:S(2)}, u32[]{:S(2)}) collective-permute-start(f32[128,288]{0,1:T(8,128)S(1)} %fusion.102), channel_id=1, source_target_pairs={{0,0},{1,1},{2,8},{3,9},{4,16},{5,17},{6,24},{7,25},{8,2},{9,3},{1... | collective-permute-start | bytes 442376 | tf_op jit(solution)/shard_map/ppermute | solution.py:158
  240.4 17.6 %collective-permute-start.21 = (f32[128,288]{0,1:T(8,128)S(1)}, f32[128,288]{0,1:T(8,128)S(1)}, u32[]{:S(2)}, u32[]{:S(2)}) collective-permute-start(f32[128,288]{0,1:T(8,128)S(1)} %fusion.104), channel_id=1, source_target_pairs={{0,0},{1,1},{2,8},{3,9},{4,16},{5,17},{6,24},{7,25},{8,2},{9,3},{1... | collective-permute-start | bytes 442376 | tf_op jit(solution)/shard_map/ppermute | solution.py:158
  245.7 14.4 %collective-permute-start.10 = (f32[128,288]{0,1:T(8,128)S(1)}, f32[128,288]{0,1:T(8,128)S(1)}, u32[]{:S(2)}, u32[]{:S(2)}) collective-permute-start(f32[128,288]{0,1:T(8,128)S(1)} %fusion.106), channel_id=1, source_target_pairs={{0,0},{1,1},{2,8},{3,9},{4,16},{5,17},{6,24},{7,25},{8,2},{9,3},{1... | collective-permute-start | bytes 442376 | tf_op jit(solution)/shard_map/ppermute | solution.py:158
  (42 other events, 388.7 us)
where the time goes:
time: 262 us; the launch traced here: 261 us
  local copies, waits for them, and re-layouts  72.3 us (28%)
  starting transfers between devices  62.1 us (24%)
  waiting for transfers between devices  44.2 us (17%)
  matrix products  40.1 us (15%)
  Pallas kernels  24.2 us (9%)
  other arithmetic  16.8 us (6%)
    concatenate x3, local copies, waits for them, and re-layouts, hidden_units(): jnp.concatenate([jnp.stack([rows_in, zeros], axis=2), jnp.stack([zeros, r...  43.1 us
    pallas_call x3, Pallas kernels, hidden_units(): pl.pallas_call(hidden_kernel, grid=(model_width // depth,), in_specs=[pl....  24.2 us
    ppermute x18, starting transfers between devices, scatter_sum(): arrived = lax.ppermute(block, 'mp', shift_permutation(count, 2, distance))  24 us
    dot_general x3, matrix products, body(): jnp.dot(gathered[layer], enc_weight[layer], preferred_element_type=jnp.fl...  15.6 us
    reshape x6, local copies, waits for them, and re-layouts, hidden_units(): spread = jnp.concatenate([jnp.stack([rows_in, zeros], axis=2), jnp.stack(...  15.5 us
    ppermute x9, starting transfers between devices, gather_inputs(): lax.ppermute(rows_in, 'mp', shift_permutation(count, 2, distance))  14.2 us
    dot_general x6, matrix products, body(): jnp.dot(latents[source], dec_weight[target * (target + 1) // 2 + source],...  13.1 us
    dot_general x3, matrix products, body(): jnp.dot(hidden, down_weight[layer], preferred_element_type=jnp.float32)  11.4 us
  transfers between devices with their start and end apart: 45, of which 19 were waited for; matrix products, arithmetic and copies ran while one was open for 47% of the time, Pallas kernels for 9%

commit v1 on v0

v1 whole, which is shorter than its diff:
```python
import functools

import jax
import jax.numpy as jnp
from jax import lax
from jax.experimental import pallas as pl
from jax.experimental.pallas import tpu as pltpu
from jax.sharding import PartitionSpec as P


def flip_permutation(count):
    return [(index, index ^ 1) for index in range(count)]


def shift_permutation(count, inner, distance):
    outer = count // inner
    return [
        (index, ((index // inner + distance) % outer) * inner + index % inner)
        for index in range(count)
    ]


def gather_inputs(rows_in, me, count):
    outer = count // 2
    position, parity = lax.div(me, 2), lax.rem(me, 2)
    parts = [rows_in] + [
        lax.ppermute(rows_in, "mp", shift_permutation(count, 2, distance))
        for distance in range(1, outer)
    ]
    around = jnp.stack([parts[(-index) % outer] for index in range(2 * outer - 1)])
    mine = lax.dynamic_slice_in_dim(around, lax.rem(outer - position, outer), outer, 0)
    other = lax.ppermute(mine, "mp", flip_permutation(count))
    even = jnp.where(parity == 0, mine, other)
    odd = jnp.where(parity == 0, other, mine)
    both = jnp.stack([even, odd], axis=1)
    chunk, rows, width = rows_in.shape
    both = both.transpose(2, 3, 0, 1, 4).reshape(chunk, rows, count * width)
    return [both[index] for index in range(chunk)]


def gather_rows(latent, me, count):
    outer = count // 2
    position, parity = lax.div(me, 2), lax.rem(me, 2)
    parts = [latent] + [
        lax.ppermute(latent, "rows", shift_permutation(count, 2, distance))
        for distance in range(1, outer)
    ]
    around = jnp.stack([parts[(-index) % outer] for index in range(2 * outer - 1)])
    mine = lax.dynamic_slice_in_dim(around, lax.rem(outer - position, outer), outer, 0)
    other = lax.ppermute(mine, "rows", flip_permutation(count))
    even = jnp.where(parity == 0, mine, other)
    odd = jnp.where(parity == 0, other, mine)
    both = jnp.stack([even, odd], axis=1)
    return both.reshape(count * latent.shape[0], latent.shape[1])


def scatter_sum(pieces, me, count):
    outer = count // 2
    position, parity = lax.div(me, 2), lax.rem(me, 2)
    split = pieces.reshape((outer, 2) + pieces.shape[1:])
    sent = jnp.where(parity == 0, split[:, 1], split[:, 0]).astype(jnp.bfloat16)
    kept = jnp.where(parity == 0, split[:, 0], split[:, 1])
    arrived = lax.ppermute(sent, "mp", flip_permutation(count))
    summed = kept + arrived.astype(jnp.float32)
    total = lax.dynamic_index_in_dim(summed, position, 0, keepdims=False)
    narrow = summed.astype(jnp.bfloat16)
    for distance in range(1, outer):
        block = lax.dynamic_index_in_dim(
            narrow, lax.rem(position + distance, outer), 0, keepdims=False
        )
        arrived = lax.ppermute(block, "mp", shift_permutation(count, 2, distance))
        total = total + arrived.astype(jnp.float32)
    return total


def hidden_kernel(rows_ref, weight_ref, hidden_ref, total_ref):
    step = pl.program_id(0)
    depth, _, columns = weight_ref.shape[1:]

    @pl.when(step == 0)
    def _():
        total_ref[...] = jnp.zeros_like(total_ref)

    weight = weight_ref[0].reshape(2 * depth, columns)
    rows_in = rows_ref[...]
    place = lax.broadcasted_iota(jnp.int32, (depth, 2 * depth), 1)
    place = place - 2 * lax.broadcasted_iota(jnp.int32, (depth, 2 * depth), 0)
    spread = jnp.concatenate(
        [
            jnp.dot(
                rows_in,
                jnp.where(place == kind, 1.0, 0.0).astype(rows_in.dtype),
                preferred_element_type=jnp.float32,
            ).astype(rows_in.dtype)
            for kind in range(2)
        ]
    )
    total_ref[...] += jnp.dot(spread, weight, preferred_element_type=jnp.float32)

    @pl.when(step == pl.num_programs(0) - 1)
    def _():
        rows = hidden_ref.shape[0]
        gate, upper = total_ref[:rows], total_ref[rows:]
        hidden = jax.nn.gelu(gate, approximate=True) * upper
        hidden_ref[...] = hidden.astype(hidden_ref.dtype)


def hidden_units(rows_in, gate_up, layer):
    rows, model_width = rows_in.shape
    hidden_local = gate_up.shape[3]
    depth = max(d for d in range(128, 385, 128) if model_width % d == 0)
    return pl.pallas_call(
        hidden_kernel,
        grid=(model_width // depth,),
        in_specs=[
            pl.BlockSpec((rows, depth), lambda step: (0, step)),
            pl.BlockSpec((1, depth, 2, hidden_local), lambda step: (layer, step, 0, 0)),
        ],
        out_specs=pl.BlockSpec((rows, hidden_local), lambda step: (0, 0)),
        out_shape=jax.ShapeDtypeStruct((rows, hidden_local), jnp.bfloat16),
        scratch_shapes=[pltpu.VMEM((2 * rows, hidden_local), jnp.float32)],
        cost_estimate=pl.CostEstimate(
            flops=8 * rows * model_width * hidden_local,
            bytes_accessed=4 * model_width * hidden_local,
            transcendentals=rows * hidden_local,
        ),
        compiler_params=pltpu.CompilerParams(vmem_limit_bytes=24 * 1024 * 1024),
    )(rows_in, gate_up)


def body(inputs, gate_up, down_weight, enc_weight, enc_bias, dec_weight):
    layers, rows, width = inputs.shape
    across, count = lax.axis_size("rows"), lax.axis_size("mp")
    my_row, me = lax.axis_index("rows"), lax.axis_index("mp")
    blocks = count // across

    gathered = gather_inputs(inputs[:1], me, count) + gather_inputs(inputs[1:], me, count)
    local = []
    for layer in range(layers):
        pre = jnp.dot(gathered[layer], enc_weight[layer], preferred_element_type=jnp.float32)
        local.append(jax.nn.relu(pre + enc_bias[layer][None, :]).astype(jnp.bfloat16))
    gathered, local = lax.optimization_barrier((gathered, local))
    latents = [gather_rows(latent, my_row, across) for latent in local]
    chunks = [range(layers - 1), range(layers - 1, layers)]
    targets = []
    for chunk in chunks:
        pieces = []
        for layer in chunk:
            hidden = hidden_units(gathered[layer], gate_up, layer)
            partial = jnp.dot(hidden, down_weight[layer], preferred_element_type=jnp.float32)
            partial = lax.optimization_barrier(partial)
            pieces.append(partial.reshape(rows, count, width).transpose(1, 0, 2))
        targets.append(scatter_sum(jnp.stack(pieces, axis=1), me, count))
    home = [
        (r * count + a * blocks + c, a * count + r * blocks + c)
        for r in range(across)
        for a in range(across)
        for c in range(blocks)
    ]
    recons = []
    for chunk in chunks:
        pieces = []
        for target in chunk:
            partial = sum(
                jnp.dot(
                    latents[source],
                    dec_weight[target * (target + 1) // 2 + source],
                    preferred_element_type=jnp.float32,
                )
                for source in range(target + 1)
            )
            blocked = partial.reshape(across, rows, blocks, width).transpose(0, 2, 1, 3)
            pieces.append(blocked.reshape(count, rows, width))
        summed = scatter_sum(jnp.stack(pieces, axis=1), me, count)
        recons.append(lax.ppermute(summed, ("rows", "mp"), home))
    recon = jnp.concatenate(recons)
    residual = jnp.concatenate(targets) - recon
    return (recon, residual)


def solution(mesh):
    in_specs = (
        P(None, "rows", "mp"),
        P(None, None, None, "mp"),
        P(None, "mp", None),
        P(None, None, "mp"),
        P(None, "mp"),
        P(None, "mp", "rows"),
    )
    out_specs = (P(None, "rows", "mp"), P(None, "rows", "mp"))
    return jax.shard_map(body, mesh=mesh, in_specs=in_specs, out_specs=out_specs, check_vma=False)
```

time: 262 us -> 234 us (0.89)
  local copies, waits for them, and re-layouts: 72.3 us -> 18.5 us
  waiting for transfers between devices: 44.2 us -> 76.2 us
  starting transfers between devices: 62.1 us -> 52.7 us
  other arithmetic: 16.8 us -> 11.5 us
  matrix products: 40.1 us -> 45.3 us
  Pallas kernels: 24.2 us -> 27.1 us
    concatenate x3 -> x1, local copies, waits for them, and re-layouts: 43.1 us -> 0.01 us  [body(): recon = jnp.concatenate(recons)]
    ppermute x3, waiting for transfers between devices: 3.59 us -> 24.3 us  [gather_rows(): lax.ppermute(latent, 'rows', shift_permutation(count, 2, distance))]
    reshape x10 -> x4, local copies, waits for them, and re-layouts: 16.8 us -> 2.22 us  [body(): blocked = partial.reshape(across, rows, blocks, width).transpose(0, 2, 1, 3)]
    ppermute x6 -> x4, waiting for transfers between devices: 5.78 us -> 15.2 us  [scatter_sum(): arrived = lax.ppermute(sent, 'mp', flip_permutation(count))]
    ppermute x3 -> x2, waiting for transfers between devices: 5.46 us -> 10.9 us  [gather_inputs(): other = lax.ppermute(mine, 'mp', flip_permutation(count))]
    pallas_call x3, Pallas kernels: 24.2 us -> 27.1 us  [hidden_units(): pl.pallas_call(hidden_kernel, grid=(model_width // depth,), in_specs=[pl....]
    ppermute x18 -> x12, waiting for transfers between devices: 10.8 us -> 7.94 us  [scatter_sum(): arrived = lax.ppermute(block, 'mp', shift_permutation(count, 2, distance))]
    ppermute x6 -> x4, starting transfers between devices: 6.65 us -> 3.97 us  [scatter_sum(): arrived = lax.ppermute(sent, 'mp', flip_permutation(count))]
  transfers between devices with their start and end apart: 45 -> 32, of which waited for: 19 -> 14; matrix products, arithmetic and copies ran while one was open for 47% -> 16% of each run, Pallas kernels for 9% -> 0%
where the time goes in v1:
time: 234 us; the launch traced here: 233 us
  waiting for transfers between devices  76.2 us (33%)
  starting transfers between devices  52.7 us (23%)
  matrix products  45.3 us (19%)
  Pallas kernels  27.1 us (12%)
  local copies, waits for them, and re-layouts  18.5 us (8%)
  other arithmetic  11.5 us (5%)
    pallas_call x3, Pallas kernels, hidden_units(): pl.pallas_call(hidden_kernel, grid=(model_width // depth,), in_specs=[pl....  27.1 us
    ppermute x3, waiting for transfers between devices, gather_rows(): lax.ppermute(latent, 'rows', shift_permutation(count, 2, distance))  24.3 us
    ppermute x12, starting transfers between devices, scatter_sum(): arrived = lax.ppermute(block, 'mp', shift_permutation(count, 2, distance))  21.4 us
    dot_general x3, matrix products, body(): jnp.dot(gathered[layer], enc_weight[layer], preferred_element_type=jnp.fl...  17.8 us
    ppermute x4, waiting for transfers between devices, scatter_sum(): arrived = lax.ppermute(sent, 'mp', flip_permutation(count))  15.2 us
    ppermute x6, starting transfers between devices, gather_inputs(): lax.ppermute(rows_in, 'mp', shift_permutation(count, 2, distance))  14.4 us
    dot_general x6, matrix products, body(): jnp.dot(latents[source], dec_weight[target * (target + 1) // 2 + source],...  14 us
    dot_general x3, matrix products, body(): jnp.dot(hidden, down_weight[layer], preferred_element_type=jnp.float32)  13.5 us
  transfers between devices with their start and end apart: 32, of which 14 were waited for; matrix products, arithmetic and copies ran while one was open for 16% of the time, Pallas kernels for 0%

profile of v1, /device:TPU:2, one launch (start us, length us, event | category | flops | bytes accessed | tf_op | source)
XLA Modules:
  0.0 232.6 jit_solution(3126047592086772014)
XLA Ops:
  1.6 3.7 %collective-permute-start.4 = (bf16[2,128,288]{1,2,0:T(8,128)(2,1)S(1)}, bf16[2,128,288]{1,2,0:T(8,128)(2,1)S(1)}, u32[]{:S(2)}, u32[]{:S(2)}) collective-permute-start(bf16[2,128,288]{1,2,0:T(8,128)(2,1)S(1)} %slice.92), channel_id=1, source_target_pairs={{0,6},{1,7},{2,0},{3,1},{4,2},{5,3},{6,4},{7,5},{8,14},{9,15},{10,... | collective-permute-start | bytes 442376 | tf_op jit(solution)/shard_map/ppermute | solution.py:27
  13.8 3.4 %collective-permute-done = bf16[1,128,288]{1,2,0:T(8,128)(2,1)S(1)} collective-permute-done((bf16[1,128,288]{1,2,0:T(8,128)(2,1)S(1)}, bf16[1,128,288]{1,2,0:T(8,128)(2,1)S(1)}, u32[]{:S(2)}, u32[]{:S(2)}) %collective-permute-start) | collective-permute-done | bytes 73760 | tf_op jit(solution)/shard_map/ppermute | solution.py:27
  17.1 5.8 %collective-permute-start.2 = (bf16[1,128,288]{1,2,0:T(8,128)(2,1)S(1)}, bf16[1,128,288]{1,2,0:T(8,128)(2,1)S(1)}, u32[]{:S(2)}, u32[]{:S(2)}) collective-permute-start(bf16[1,128,288]{1,2,0:T(8,128)(2,1)S(1)} %slice.91), channel_id=1, source_target_pairs={{0,2},{1,3},{2,4},{3,5},{4,6},{5,7},{6,0},{7,1},{8,10},{9,11},{10,... | collective-permute-start | bytes 221192 | tf_op jit(solution)/shard_map/ppermute | solution.py:27
  27.4 7.6 %collective-permute-done.3 = bf16[4,1,128,288]{2,3,0,1:T(8,128)(2,1)S(1)} collective-permute-done((bf16[4,1,128,288]{2,3,0,1:T(8,128)(2,1)S(1)}, bf16[4,1,128,288]{2,3,0,1:T(8,128)(2,1)S(1)}, u32[]{:S(2)}, u32[]{:S(2)}) %collective-permute-start.3) | collective-permute-done | bytes 294944 | tf_op jit(solution)/shard_map/ppermute | solution.py:32
  35.1 5.9 %fusion.42 = bf16[128,2048]{1,0:T(8,128)(2,1)} fusion(bf16[128,2304]{0,1:T(8,128)(2,1)S(1)} %bitcast.313, bf16[3,2304,2048]{2,1,0:T(8,128)(2,1)} %param.9, f32[2048]{0:T(1024)S(1)} %bitcast.339), kind=kOutput, calls=%fused_computation.26 | convolution fusion | flops 1208745984 | bytes 10559488 | tf_op jit(solution)/shard_map/dot_general | solution.py:140
  41.0 3.3 %collective-permute-done.7 = bf16[4,2,128,288]{2,3,0,1:T(8,128)(2,1)S(1)} collective-permute-done((bf16[4,2,128,288]{2,3,0,1:T(8,128)(2,1)S(1)}, bf16[4,2,128,288]{2,3,0,1:T(8,128)(2,1)S(1)}, u32[]{:S(2)}, u32[]{:S(2)}) %collective-permute-start.7) | collective-permute-done | bytes 589856 | tf_op jit(solution)/shard_map/ppermute | solution.py:32
  44.7 5.9 %fusion.36 = bf16[128,2048]{1,0:T(8,128)(2,1)} fusion(bf16[128,2304]{0,1:T(8,128)(2,1)S(1)} %bitcast.315, bf16[3,2304,2048]{2,1,0:T(8,128)(2,1)} %param.9, f32[2048]{0:T(1024)S(1)} %bitcast.338), kind=kOutput, calls=%fused_computation.24 | convolution fusion | flops 1208745984 | bytes 10559488 | tf_op jit(solution)/shard_map/dot_general | solution.py:140
  50.6 6.0 %fusion.39 = bf16[128,2048]{1,0:T(8,128)(2,1)} fusion(bf16[128,2304]{0,1:T(8,128)(2,1)S(1)} %bitcast.317, bf16[3,2304,2048]{2,1,0:T(8,128)(2,1)} %param.9, f32[2048]{0:T(1024)S(1)} %bitcast.337), kind=kOutput, calls=%fused_computation.25 | convolution fusion | flops 1208745984 | bytes 10559488 | tf_op jit(solution)/shard_map/dot_general | solution.py:140
  56.8 9.1 %shard_map.77 = bf16[128,1152]{1,0:T(8,128)(2,1)S(1)} custom-call(bf16[128,2304]{1,0:T(8,128)(2,1)S(1)} %copy.46.rows_ref, bf16[3,2304,2,1152]{3,2,1,0:T(2,128)(2,1)} %weight_ref.5), custom_call_target="tpu_custom_call" | custom-call | flops 2717908992 | bytes 10616832 | tf_op jit(solution)/shard_map/pallas_call | solution.py:112
  66.0 4.5 %fusion.13 = f32[128,2304]{1,0:T(8,128)} fusion(bf16[128,1152]{1,0:T(8,128)(2,1)S(1)} %shard_map.77, bf16[3,1152,2304]{2,1,0:T(8,128)(2,1)} %param.8), kind=kOutput, calls=%fused_computation.13 | convolution fusion | flops 679477248 | bytes 6782976 | tf_op jit(solution)/shard_map/dot_general | solution.py:150
  72.4 9.0 %shard_map.78 = bf16[128,1152]{1,0:T(8,128)(2,1)S(1)} custom-call(bf16[128,2304]{1,0:T(8,128)(2,1)S(1)} %copy.48.rows_ref, bf16[3,2304,2,1152]{3,2,1,0:T(2,128)(2,1)} %weight_ref.5), custom_call_target="tpu_custom_call" | custom-call | flops 2717908992 | bytes 10616832 | tf_op jit(solution)/shard_map/pallas_call | solution.py:112
  81.3 4.5 %fusion.11 = f32[128,2304]{1,0:T(8,128)} fusion(bf16[128,1152]{1,0:T(8,128)(2,1)S(1)} %shard_map.78, bf16[3,1152,2304]{2,1,0:T(8,128)(2,1)} %param.8), kind=kOutput, calls=%fused_computation.11 | convolution fusion | flops 679477248 | bytes 6782976 | tf_op jit(solution)/shard_map/dot_general | solution.py:150
  87.7 9.0 %shard_map.79 = bf16[128,1152]{1,0:T(8,128)(2,1)S(1)} custom-call(bf16[128,2304]{1,0:T(8,128)(2,1)S(1)} %copy.52.rows_ref, bf16[3,2304,2,1152]{3,2,1,0:T(2,128)(2,1)} %weight_ref.5), custom_call_target="tpu_custom_call" | custom-call | flops 2717908992 | bytes 10616832 | tf_op jit(solution)/shard_map/pallas_call | solution.py:112
  96.7 4.5 %fusion.9 = f32[128,2304]{1,0:T(8,128)} fusion(bf16[128,1152]{1,0:T(8,128)(2,1)S(1)} %shard_map.79, bf16[3,1152,2304]{2,1,0:T(8,128)(2,1)} %param.8), kind=kOutput, calls=%fused_computation.9 | convolution fusion | flops 679477248 | bytes 6782976 | tf_op jit(solution)/shard_map/dot_general | solution.py:150
  113.3 24.3 %collective-permute-done.10 = bf16[128,2048]{1,0:T(8,128)(2,1)S(1)} collective-permute-done((bf16[128,2048]{1,0:T(8,128)(2,1)}, bf16[128,2048]{1,0:T(8,128)(2,1)S(1)}, u32[]{:S(2)}, u32[]{:S(2)}) %collective-permute-start.10) | collective-permute-done | bytes 524320 | tf_op jit(solution)/shard_map/ppermute | solution.py:45
  144.9 7.2 %collective-permute-done.24 = bf16[4,2,128,288]{2,3,0,1:T(8,128)(2,1)S(1)} collective-permute-done((bf16[4,2,128,288]{2,3,0,1:T(8,128)(2,1)S(1)}, bf16[4,2,128,288]{2,3,0,1:T(8,128)(2,1)S(1)}, u32[]{:S(2)}, u32[]{:S(2)}) %collective-permute-start.24) | collective-permute-done | bytes 589856 | tf_op jit(solution)/shard_map/ppermute | solution.py:63
  154.1 4.3 %collective-permute-start.26 = (bf16[2,128,288]{1,2,0:T(8,128)(2,1)}, bf16[2,128,288]{1,2,0:T(8,128)(2,1)}, u32[]{:S(2)}, u32[]{:S(2)}) collective-permute-start(bf16[2,128,288]{1,2,0:T(8,128)(2,1)} %get-tuple-element.36), channel_id=1, source_target_pairs={{0,4},{1,5},{2,6},{3,7},{4,0},{5,1},{6,2},{7,3},{8,12},{9,13},{10,... | collective-permute-start | bytes 442376 | tf_op jit(solution)/shard_map/ppermute | solution.py:71
  172.8 3.2 %convolution_bitcast_fusion = f32[4,2,1,128,288]{3,4,1,0,2:T(8,128)S(1)} fusion(bf16[4,128,2048,1]{2,1,3,0:T(8,128)(2,1)} %bitcast.334, bf16[2,288,2048,1]{2,1,0,3:T(8,128)(2,1)S(1)} %bitcast.312), kind=kOutput, calls=%fused_computation.58 | convolution fusion | flops 1207959552 | bytes 5636096 | tf_op jit(solution)/shard_map/dot_general | solution.py:165
  177.8 4.1 %fusion.66 = f32[512,576]{0,1:T(8,128)} fusion(f32[512,576]{0,1:T(8,128)S(1)} %copy-done.9, f32[512,576]{0,1:T(8,128)S(1)} %fusion.47, bf16[512,2048]{1,0:T(8,128)(2,1)S(1)} %bitcast.335, bf16[6,2048,576]{1,2,0:T(8,128)(2,1)} %param.11), kind=kOutput, calls=%fused_computation.61 | convolution fusion | flops 1208549376 | bytes 7995392 | tf_op jit(solution)/shard_map/dot_general | solution.py:165
  185.1 5.7 %collective-permute-done.12 = bf16[4,2,128,288]{2,3,0,1:T(8,128)(2,1)} collective-permute-done((bf16[4,2,128,288]{2,3,0,1:T(8,128)(2,1)}, bf16[4,2,128,288]{2,3,0,1:T(8,128)(2,1)}, u32[]{:S(2)}, u32[]{:S(2)}) %collective-permute-start.12) | collective-permute-done | bytes 589856 | tf_op jit(solution)/shard_map/ppermute | solution.py:63
  196.1 4.4 %collective-permute-done.13 = bf16[2,128,288]{1,2,0:T(8,128)(2,1)S(1)} collective-permute-done((bf16[2,128,288]{1,2,0:T(8,128)(2,1)S(1)}, bf16[2,128,288]{1,2,0:T(8,128)(2,1)S(1)}, u32[]{:S(2)}, u32[]{:S(2)}) %collective-permute-start.13) | collective-permute-done | bytes 147488 | tf_op jit(solution)/shard_map/ppermute | solution.py:71
  204.5 4.2 %collective-permute-start.22 = (bf16[1,128,288]{1,2,0:T(8,128)(2,1)S(1)}, bf16[1,128,288]{1,2,0:T(8,128)(2,1)S(1)}, u32[]{:S(2)}, u32[]{:S(2)}) collective-permute-start(bf16[1,128,288]{1,2,0:T(8,128)(2,1)S(1)} %get-tuple-element.46), channel_id=1, source_target_pairs={{0,6},{1,7},{2,0},{3,1},{4,2},{5,3},{6,4},{7,5},{8,14},{9,15},{10,... | collective-permute-start | bytes 221192 | tf_op jit(solution)/shard_map/ppermute | solution.py:71
  210.2 5.3 %collective-permute-start.16 = (f32[2,128,288]{1,2,0:T(8,128)S(1)}, f32[2,128,288]{1,2,0:T(8,128)S(1)}, u32[]{:S(2)}, u32[]{:S(2)}) collective-permute-start(f32[2,128,288]{1,2,0:T(8,128)S(1)} %fusion.86), channel_id=1, source_target_pairs={{0,0},{1,1},{2,8},{3,9},{4,16},{5,17},{6,24},{7,25},{8,2},{9,3},{1... | collective-permute-start | bytes 884744 | tf_op jit(solution)/shard_map/ppermute | solution.py:175
  219.2 9.9 %collective-permute-done.16 = f32[2,128,288]{1,2,0:T(8,128)S(1)} collective-permute-done((f32[2,128,288]{1,2,0:T(8,128)S(1)}, f32[2,128,288]{1,2,0:T(8,128)S(1)}, u32[]{:S(2)}, u32[]{:S(2)}) %collective-permute-start.16) | collective-permute-done | bytes 294944 | tf_op jit(solution)/shard_map/ppermute | solution.py:175
  (152 shorter events, 76.6 us)
Async XLA Ops:
  1.6 25.1 %collective-permute-start.4 = (bf16[2,128,288]{1,2,0:T(8,128)(2,1)S(1)}, bf16[2,128,288]{1,2,0:T(8,128)(2,1)S(1)}, u32[]{:S(2)}, u32[]{:S(2)}) collective-permute-start(bf16[2,128,288]{1,2,0:T(8,128)(2,1)S(1)} %slice.92), channel_id=1, source_target_pairs={{0,6},{1,7},{2,0},{3,1},{4,2},{5,3},{6,4},{7,5},{8,14},{9,15},{10,... | collective-permute-start | bytes 442376 | tf_op jit(solution)/shard_map/ppermute | solution.py:27
  5.2 21.4 %collective-permute-start.5 = (bf16[2,128,288]{1,2,0:T(8,128)(2,1)S(1)}, bf16[2,128,288]{1,2,0:T(8,128)(2,1)S(1)}, u32[]{:S(2)}, u32[]{:S(2)}) collective-permute-start(bf16[2,128,288]{1,2,0:T(8,128)(2,1)S(1)} %slice.92), channel_id=1, source_target_pairs={{0,4},{1,5},{2,6},{3,7},{4,0},{5,1},{6,2},{7,3},{8,12},{9,13},{10,... | collective-permute-start | bytes 442376 | tf_op jit(solution)/shard_map/ppermute | solution.py:27
  5.2 21.5 %collective-permute-start.6 = (bf16[2,128,288]{1,2,0:T(8,128)(2,1)S(1)}, bf16[2,128,288]{1,2,0:T(8,128)(2,1)S(1)}, u32[]{:S(2)}, u32[]{:S(2)}) collective-permute-start(bf16[2,128,288]{1,2,0:T(8,128)(2,1)S(1)} %slice.92), channel_id=1, source_target_pairs={{0,2},{1,3},{2,4},{3,5},{4,6},{5,7},{6,0},{7,1},{8,10},{9,11},{10,... | collective-permute-start | bytes 442376 | tf_op jit(solution)/shard_map/ppermute | solution.py:27
  7.1 10.0 %collective-permute-start = (bf16[1,128,288]{1,2,0:T(8,128)(2,1)S(1)}, bf16[1,128,288]{1,2,0:T(8,128)(2,1)S(1)}, u32[]{:S(2)}, u32[]{:S(2)}) collective-permute-start(bf16[1,128,288]{1,2,0:T(8,128)(2,1)S(1)} %slice.91), channel_id=1, source_target_pairs={{0,6},{1,7},{2,0},{3,1},{4,2},{5,3},{6,4},{7,5},{8,14},{9,15},{10,... | collective-permute-start | bytes 221192 | tf_op jit(solution)/shard_map/ppermute | solution.py:27
  9.9 14.1 %collective-permute-start.1 = (bf16[1,128,288]{1,2,0:T(8,128)(2,1)S(1)}, bf16[1,128,288]{1,2,0:T(8,128)(2,1)S(1)}, u32[]{:S(2)}, u32[]{:S(2)}) collective-permute-start(bf16[1,128,288]{1,2,0:T(8,128)(2,1)S(1)} %slice.91), channel_id=1, source_target_pairs={{0,4},{1,5},{2,6},{3,7},{4,0},{5,1},{6,2},{7,3},{8,12},{9,13},{10,... | collective-permute-start | bytes 221192 | tf_op jit(solution)/shard_map/ppermute | solution.py:27
  26.9 17.5 %collective-permute-start.7 = (bf16[4,2,128,288]{2,3,0,1:T(8,128)(2,1)S(1)}, bf16[4,2,128,288]{2,3,0,1:T(8,128)(2,1)S(1)}, u32[]{:S(2)}, u32[]{:S(2)}) collective-permute-start(bf16[4,2,128,288]{2,3,0,1:T(8,128)(2,1)S(1)} %constant_dynamic-slice_fusion), channel_id=1, source_target_pairs={{0,1},{1,0},{2,3},{3,2},{4,5},{5,4},{6,7},{7,6},{8,9},{9,8},{10,11... | collective-permute-start | bytes 1769480 | tf_op jit(solution)/shard_map/ppermute | solution.py:32
  104.5 38.6 %collective-permute-start.17 = (bf16[128,2048]{1,0:T(8,128)(2,1)}, bf16[128,2048]{1,0:T(8,128)(2,1)S(1)}, u32[]{:S(2)}, u32[]{:S(2)}) collective-permute-start(bf16[128,2048]{1,0:T(8,128)(2,1)} %fusion.36), channel_id=1, source_target_pairs={{0,16},{8,24},{16,0},{24,8},{1,17},{9,25},{17,1},{25,9},{2,18},{10... | collective-permute-start | bytes 1572872 | tf_op jit(solution)/shard_map/ppermute | solution.py:45
  105.0 38.7 %collective-permute-start.8 = (bf16[128,2048]{1,0:T(8,128)(2,1)}, bf16[128,2048]{1,0:T(8,128)(2,1)S(1)}, u32[]{:S(2)}, u32[]{:S(2)}) collective-permute-start(bf16[128,2048]{1,0:T(8,128)(2,1)} %fusion.42), channel_id=1, source_target_pairs={{0,16},{8,24},{16,0},{24,8},{1,17},{9,25},{17,1},{25,9},{2,18},{10... | collective-permute-start | bytes 1572872 | tf_op jit(solution)/shard_map/ppermute | solution.py:45
  106.5 31.0 %collective-permute-start.10 = (bf16[128,2048]{1,0:T(8,128)(2,1)}, bf16[128,2048]{1,0:T(8,128)(2,1)S(1)}, u32[]{:S(2)}, u32[]{:S(2)}) collective-permute-start(bf16[128,2048]{1,0:T(8,128)(2,1)} %fusion.39), channel_id=1, source_target_pairs={{0,16},{8,24},{16,0},{24,8},{1,17},{9,25},{17,1},{25,9},{2,18},{10... | collective-permute-start | bytes 1572872 | tf_op jit(solution)/shard_map/ppermute | solution.py:45
  109.8 31.1 %collective-permute-start.29 = (bf16[1,128,288]{1,2,0:T(8,128)(2,1)S(1)}, bf16[1,128,288]{1,2,0:T(8,128)(2,1)S(1)}, u32[]{:S(2)}, u32[]{:S(2)}) collective-permute-start(bf16[1,128,288]{1,2,0:T(8,128)(2,1)S(1)} %get-tuple-element.42), channel_id=1, source_target_pairs={{0,2},{1,3},{2,4},{3,5},{4,6},{5,7},{6,0},{7,1},{8,10},{9,11},{10,... | collective-permute-start | bytes 221192 | tf_op jit(solution)/shard_map/ppermute | solution.py:71
  111.4 30.2 %collective-permute-start.30 = (bf16[1,128,288]{1,2,0:T(8,128)(2,1)S(1)}, bf16[1,128,288]{1,2,0:T(8,128)(2,1)S(1)}, u32[]{:S(2)}, u32[]{:S(2)}) collective-permute-start(bf16[1,128,288]{1,2,0:T(8,128)(2,1)S(1)} %get-tuple-element.44), channel_id=1, source_target_pairs={{0,4},{1,5},{2,6},{3,7},{4,0},{5,1},{6,2},{7,3},{8,12},{9,13},{10,... | collective-permute-start | bytes 221192 | tf_op jit(solution)/shard_map/ppermute | solution.py:71
  141.0 11.0 %collective-permute-start.24 = (bf16[4,2,128,288]{2,3,0,1:T(8,128)(2,1)S(1)}, bf16[4,2,128,288]{2,3,0,1:T(8,128)(2,1)S(1)}, u32[]{:S(2)}, u32[]{:S(2)}) collective-permute-start(bf16[4,2,128,288]{2,3,0,1:T(8,128)(2,1)S(1)} %fusion.80), channel_id=1, source_target_pairs={{0,1},{1,0},{2,3},{3,2},{4,5},{5,4},{6,7},{7,6},{8,9},{9,8},{10,11... | collective-permute-start | bytes 1769480 | tf_op jit(solution)/shard_map/ppermute | solution.py:63
  141.6 16.8 %collective-permute-start.11 = (bf16[2,128,2048]{2,1,0:T(8,128)(2,1)S(1)}, bf16[2,128,2048]{2,1,0:T(8,128)(2,1)S(1)}, u32[]{:S(2)}, u32[]{:S(2)}) collective-permute-start(bf16[2,128,2048]{2,1,0:T(8,128)(2,1)S(1)} %fusion.76), channel_id=1, source_target_pairs={{0,8},{8,0},{16,24},{24,16},{1,9},{9,1},{17,25},{25,17},{2,10},{10... | collective-permute-start | bytes 3145736 | tf_op jit(solution)/shard_map/ppermute | solution.py:50
  143.6 18.2 %collective-permute-start.18 = (bf16[2,128,2048]{2,1,0:T(8,128)(2,1)S(1)}, bf16[2,128,2048]{2,1,0:T(8,128)(2,1)S(1)}, u32[]{:S(2)}, u32[]{:S(2)}) collective-permute-start(bf16[2,128,2048]{2,1,0:T(8,128)(2,1)S(1)} %fusion.74), channel_id=1, source_target_pairs={{0,8},{8,0},{16,24},{24,16},{1,9},{9,1},{17,25},{25,17},{2,10},{10... | collective-permute-start | bytes 3145736 | tf_op jit(solution)/shard_map/ppermute | solution.py:50
  144.3 22.5 %collective-permute-start.9 = (bf16[2,128,2048]{2,1,0:T(8,128)(2,1)S(1)}, bf16[2,128,2048]{2,1,0:T(8,128)(2,1)S(1)}, u32[]{:S(2)}, u32[]{:S(2)}) collective-permute-start(bf16[2,128,2048]{2,1,0:T(8,128)(2,1)S(1)} %fusion.78), channel_id=1, source_target_pairs={{0,8},{8,0},{16,24},{24,16},{1,9},{9,1},{17,25},{25,17},{2,10},{10... | collective-permute-start | bytes 3145736 | tf_op jit(solution)/shard_map/ppermute | solution.py:50
  154.0 63.9 %collective-permute-start.25 = (bf16[2,128,288]{1,2,0:T(8,128)(2,1)}, bf16[2,128,288]{1,2,0:T(8,128)(2,1)}, u32[]{:S(2)}, u32[]{:S(2)}) collective-permute-start(bf16[2,128,288]{1,2,0:T(8,128)(2,1)} %get-tuple-element.34), channel_id=1, source_target_pairs={{0,2},{1,3},{2,4},{3,5},{4,6},{5,7},{6,0},{7,1},{8,10},{9,11},{10,... | collective-permute-start | bytes 442376 | tf_op jit(solution)/shard_map/ppermute | solution.py:71
  154.1 63.9 %collective-permute-start.26 = (bf16[2,128,288]{1,2,0:T(8,128)(2,1)}, bf16[2,128,288]{1,2,0:T(8,128)(2,1)}, u32[]{:S(2)}, u32[]{:S(2)}) collective-permute-start(bf16[2,128,288]{1,2,0:T(8,128)(2,1)} %get-tuple-element.36), channel_id=1, source_target_pairs={{0,4},{1,5},{2,6},{3,7},{4,0},{5,1},{6,2},{7,3},{8,12},{9,13},{10,... | collective-permute-start | bytes 442376 | tf_op jit(solution)/shard_map/ppermute | solution.py:71
  177.0 13.8 %collective-permute-start.12 = (bf16[4,2,128,288]{2,3,0,1:T(8,128)(2,1)}, bf16[4,2,128,288]{2,3,0,1:T(8,128)(2,1)}, u32[]{:S(2)}, u32[]{:S(2)}) collective-permute-start(bf16[4,2,128,288]{2,3,0,1:T(8,128)(2,1)} %fusion.79), channel_id=1, source_target_pairs={{0,1},{1,0},{2,3},{3,2},{4,5},{5,4},{6,7},{7,6},{8,9},{9,8},{10,11... | collective-permute-start | bytes 1769480 | tf_op jit(solution)/shard_map/ppermute | solution.py:63
  183.8 10.4 %collective-permute-start.19 = (bf16[4,1,128,288]{2,3,1,0:T(8,128)(2,1)S(1)}, bf16[4,1,128,288]{2,3,1,0:T(8,128)(2,1)S(1)}, u32[]{:S(2)}, u32[]{:S(2)}) collective-permute-start(bf16[4,1,128,288]{2,3,1,0:T(8,128)(2,1)S(1)} %fusion.81), channel_id=1, source_target_pairs={{0,1},{1,0},{2,3},{3,2},{4,5},{5,4},{6,7},{7,6},{8,9},{9,8},{10,11... | collective-permute-start | bytes 884744 | tf_op jit(solution)/shard_map/ppermute | solution.py:63
  192.4 10.8 %collective-permute-start.14 = (bf16[2,128,288]{1,2,0:T(8,128)(2,1)S(1)}, bf16[2,128,288]{1,2,0:T(8,128)(2,1)S(1)}, u32[]{:S(2)}, u32[]{:S(2)}) collective-permute-start(bf16[2,128,288]{1,2,0:T(8,128)(2,1)S(1)} %get-tuple-element.39), channel_id=1, source_target_pairs={{0,4},{1,5},{2,6},{3,7},{4,0},{5,1},{6,2},{7,3},{8,12},{9,13},{10,... | collective-permute-start | bytes 442376 | tf_op jit(solution)/shard_map/ppermute | solution.py:71
  194.2 10.3 %collective-permute-start.15 = (bf16[2,128,288]{1,2,0:T(8,128)(2,1)S(1)}, bf16[2,128,288]{1,2,0:T(8,128)(2,1)S(1)}, u32[]{:S(2)}, u32[]{:S(2)}) collective-permute-start(bf16[2,128,288]{1,2,0:T(8,128)(2,1)S(1)} %get-tuple-element.38), channel_id=1, source_target_pairs={{0,6},{1,7},{2,0},{3,1},{4,2},{5,3},{6,4},{7,5},{8,14},{9,15},{10,... | collective-permute-start | bytes 442376 | tf_op jit(solution)/shard_map/ppermute | solution.py:71
  204.5 11.1 %collective-permute-start.22 = (bf16[1,128,288]{1,2,0:T(8,128)(2,1)S(1)}, bf16[1,128,288]{1,2,0:T(8,128)(2,1)S(1)}, u32[]{:S(2)}, u32[]{:S(2)}) collective-permute-start(bf16[1,128,288]{1,2,0:T(8,128)(2,1)S(1)} %get-tuple-element.46), channel_id=1, source_target_pairs={{0,6},{1,7},{2,0},{3,1},{4,2},{5,3},{6,4},{7,5},{8,14},{9,15},{10,... | collective-permute-start | bytes 221192 | tf_op jit(solution)/shard_map/ppermute | solution.py:71
  210.2 18.9 %collective-permute-start.16 = (f32[2,128,288]{1,2,0:T(8,128)S(1)}, f32[2,128,288]{1,2,0:T(8,128)S(1)}, u32[]{:S(2)}, u32[]{:S(2)}) collective-permute-start(f32[2,128,288]{1,2,0:T(8,128)S(1)} %fusion.86), channel_id=1, source_target_pairs={{0,0},{1,1},{2,8},{3,9},{4,16},{5,17},{6,24},{7,25},{8,2},{9,3},{1... | collective-permute-start | bytes 884744 | tf_op jit(solution)/shard_map/ppermute | solution.py:175
  215.6 16.0 %collective-permute-start.23 = (f32[1,128,288]{1,2,0:T(8,128)S(1)}, f32[1,128,288]{1,2,0:T(8,128)S(1)}, u32[]{:S(2)}, u32[]{:S(2)}) collective-permute-start(f32[1,128,288]{1,2,0:T(8,128)S(1)} %fusion.90), channel_id=1, source_target_pairs={{0,0},{1,1},{2,8},{3,9},{4,16},{5,17},{6,24},{7,25},{8,2},{9,3},{1... | collective-permute-start | bytes 442376 | tf_op jit(solution)/shard_map/ppermute | solution.py:175
  (23 other events, 278.5 us)

commit v2 on v1

--- a/solution.py
+++ b/solution.py
@@ -51,7 +51,8 @@
     even = jnp.where(parity == 0, mine, other)
     odd = jnp.where(parity == 0, other, mine)
     both = jnp.stack([even, odd], axis=1)
-    return both.reshape(count * latent.shape[0], latent.shape[1])
+    layers, rows, width = latent.shape
+    return [both[:, :, layer].reshape(count * rows, width) for layer in range(layers)]
 
 
 def scatter_sum(pieces, me, count):
@@ -139,8 +140,8 @@
     for layer in range(layers):
         pre = jnp.dot(gathered[layer], enc_weight[layer], preferred_element_type=jnp.float32)
         local.append(jax.nn.relu(pre + enc_bias[layer][None, :]).astype(jnp.bfloat16))
-    gathered, local = lax.optimization_barrier((gathered, local))
-    latents = [gather_rows(latent, my_row, across) for latent in local]
+    gathered, local = lax.optimization_barrier((gathered, jnp.stack(local)))
+    latents = gather_rows(local, my_row, across)
     chunks = [range(layers - 1), range(layers - 1, layers)]
     targets = []
     for chunk in chunks:

time: 234 us -> 238 us (1.017)
  other arithmetic: 11.5 us -> 21.6 us
  waiting for transfers between devices: 76.2 us -> 70.7 us
  local copies, waits for them, and re-layouts: 18.5 us -> 21.8 us
  matrix products: 45.3 us -> 42 us
    ppermute x3 -> x1, waiting for transfers between devices: 24.3 us -> 15.7 us  [gather_rows(): lax.ppermute(latent, 'rows', shift_permutation(count, 2, distance))]
    another operation x3 -> x1, other arithmetic: 1.7 us -> 4.81 us  [gather_rows(): jnp.stack([parts[-index % outer] for index in range(2 * outer - 1)])]
    unnamed x41 -> x45, local copies, waits for them, and re-layouts: 4.61 us -> 6.26 us
  transfers between devices with their start and end apart: 32 -> 28, of which waited for: 14 -> 16; matrix products, arithmetic and copies ran while one was open for 16% -> 27% of each run, Pallas kernels for 0% -> 11%
where the time goes in v2:
time: 238 us; the launch traced here: 237 us
  waiting for transfers between devices  70.7 us (30%)
  starting transfers between devices  52.6 us (22%)
  matrix products  42 us (18%)
  Pallas kernels  27 us (11%)
  local copies, waits for them, and re-layouts  21.8 us (9%)
  other arithmetic  21.6 us (9%)
    pallas_call x3, Pallas kernels, hidden_units(): pl.pallas_call(hidden_kernel, grid=(model_width // depth,), in_specs=[pl....  27 us
    ppermute x12, starting transfers between devices, scatter_sum(): arrived = lax.ppermute(block, 'mp', shift_permutation(count, 2, distance))  22.9 us
    ppermute x1, waiting for transfers between devices, gather_rows(): lax.ppermute(latent, 'rows', shift_permutation(count, 2, distance))  15.7 us
    dot_general x3, matrix products, body(): jnp.dot(gathered[layer], enc_weight[layer], preferred_element_type=jnp.fl...  15.5 us
    ppermute x2, waiting for transfers between devices, body(): recons.append(lax.ppermute(summed, ('rows', 'mp'), home))  14.7 us
    ppermute x6, starting transfers between devices, gather_inputs(): lax.ppermute(rows_in, 'mp', shift_permutation(count, 2, distance))  14.4 us
    dot_general x6, matrix products, body(): jnp.dot(latents[source], dec_weight[target * (target + 1) // 2 + source],...  14 us
    ppermute x4, waiting for transfers between devices, scatter_sum(): arrived = lax.ppermute(sent, 'mp', flip_permutation(count))  13.3 us
  transfers between devices with their start and end apart: 28, of which 16 were waited for; matrix products, arithmetic and copies ran while one was open for 27% of the time, Pallas kernels for 11%

profile of v2, /device:TPU:2, one launch (start us, length us, event | category | flops | bytes accessed | tf_op | source)
XLA Modules:
  0.0 236.9 jit_solution(15100227224133220304)
XLA Ops:
  1.6 3.7 %collective-permute-start.4 = (bf16[2,128,288]{1,2,0:T(8,128)(2,1)S(1)}, bf16[2,128,288]{1,2,0:T(8,128)(2,1)S(1)}, u32[]{:S(2)}, u32[]{:S(2)}) collective-permute-start(bf16[2,128,288]{1,2,0:T(8,128)(2,1)S(1)} %slice.101), channel_id=1, source_target_pairs={{0,6},{1,7},{2,0},{3,1},{4,2},{5,3},{6,4},{7,5},{8,14},{9,15},{10,... | collective-permute-start | bytes 442376 | tf_op jit(solution)/shard_map/ppermute | solution.py:27
  17.2 5.8 %collective-permute-start.2 = (bf16[1,128,288]{1,2,0:T(8,128)(2,1)S(1)}, bf16[1,128,288]{1,2,0:T(8,128)(2,1)S(1)}, u32[]{:S(2)}, u32[]{:S(2)}) collective-permute-start(bf16[1,128,288]{1,2,0:T(8,128)(2,1)S(1)} %slice.100), channel_id=1, source_target_pairs={{0,2},{1,3},{2,4},{3,5},{4,6},{5,7},{6,0},{7,1},{8,10},{9,11},{10,... | collective-permute-start | bytes 221192 | tf_op jit(solution)/shard_map/ppermute | solution.py:27
  28.4 7.6 %collective-permute-done.3 = bf16[4,1,128,288]{2,3,0,1:T(8,128)(2,1)S(1)} collective-permute-done((bf16[4,1,128,288]{2,3,0,1:T(8,128)(2,1)S(1)}, bf16[4,1,128,288]{2,3,0,1:T(8,128)(2,1)S(1)}, u32[]{:S(2)}, u32[]{:S(2)}) %collective-permute-start.3) | collective-permute-done | bytes 294944 | tf_op jit(solution)/shard_map/ppermute | solution.py:32
  36.1 5.1 %fusion.62 = bf16[1,128,2048]{2,1,0:T(8,128)(2,1)S(1)} fusion(bf16[128,2304]{0,1:T(8,128)(2,1)S(1)} %bitcast.315, bf16[3,2304,2048]{2,1,0:T(8,128)(2,1)} %param.9, f32[2048]{0:T(1024)S(1)} %bitcast.329), kind=kOutput, calls=%fused_computation.57 | convolution fusion | flops 1208745984 | bytes 10559488 | tf_op jit(solution)/shard_map/dot_general | solution.py:141
  41.2 4.1 %collective-permute-done.7 = bf16[4,2,128,288]{2,3,0,1:T(8,128)(2,1)S(1)} collective-permute-done((bf16[4,2,128,288]{2,3,0,1:T(8,128)(2,1)S(1)}, bf16[4,2,128,288]{2,3,0,1:T(8,128)(2,1)S(1)}, u32[]{:S(2)}, u32[]{:S(2)}) %collective-permute-start.7) | collective-permute-done | bytes 589856 | tf_op jit(solution)/shard_map/ppermute | solution.py:32
  45.6 5.3 %fusion.65 = bf16[1,128,2048]{2,1,0:T(8,128)(2,1)S(1)} fusion(bf16[128,2304]{0,1:T(8,128)(2,1)S(1)} %bitcast.319, bf16[3,2304,2048]{2,1,0:T(8,128)(2,1)} %param.9, f32[2048]{0:T(1024)S(1)} %bitcast.328), kind=kOutput, calls=%fused_computation.58 | convolution fusion | flops 1208745984 | bytes 10559488 | tf_op jit(solution)/shard_map/dot_general | solution.py:141
  51.0 5.1 %fusion.68 = bf16[1,128,2048]{2,1,0:T(8,128)(2,1)S(1)} fusion(bf16[128,2304]{0,1:T(8,128)(2,1)S(1)} %bitcast.317, bf16[3,2304,2048]{2,1,0:T(8,128)(2,1)} %param.9, f32[2048]{0:T(1024)S(1)} %bitcast.327), kind=kOutput, calls=%fused_computation.59 | convolution fusion | flops 1208745984 | bytes 10559488 | tf_op jit(solution)/shard_map/dot_general | solution.py:141
  57.1 9.1 %shard_map.77 = bf16[128,1152]{1,0:T(8,128)(2,1)S(1)} custom-call(bf16[128,2304]{1,0:T(8,128)(2,1)S(1)} %copy.46.rows_ref, bf16[3,2304,2,1152]{3,2,1,0:T(2,128)(2,1)} %weight_ref.5), custom_call_target="tpu_custom_call" | custom-call | flops 2717908992 | bytes 10616832 | tf_op jit(solution)/shard_map/pallas_call | solution.py:113
  66.3 4.5 %fusion.13 = f32[128,2304]{1,0:T(8,128)} fusion(bf16[128,1152]{1,0:T(8,128)(2,1)S(1)} %shard_map.77, bf16[3,1152,2304]{2,1,0:T(8,128)(2,1)} %param.8), kind=kOutput, calls=%fused_computation.17 | convolution fusion | flops 679477248 | bytes 6782976 | tf_op jit(solution)/shard_map/dot_general | solution.py:151
  73.8 15.7 %collective-permute-done.8 = bf16[3,128,2048]{2,1,0:T(8,128)(2,1)} collective-permute-done((bf16[3,128,2048]{2,1,0:T(8,128)(2,1)S(1)}, bf16[3,128,2048]{2,1,0:T(8,128)(2,1)}, u32[]{:S(2)}, u32[]{:S(2)}) %collective-permute-start.8) | collective-permute-done | bytes 1572896 | tf_op jit(solution)/shard_map/ppermute | solution.py:45
  89.5 4.8 %fusion.19 = bf16[2,3,128,2048]{3,2,1,0:T(8,128)(2,1)} fusion(s32[]{:T(128)S(6)} %select_n.168, bf16[1,3,128,2048]{3,2,1,0:T(8,128)(2,1)S(1)} %bitcast.302, bf16[1,3,128,2048]{3,2,1,0:T(8,128)(2,1)} %bitcast.40), kind=kLoop, calls=%fused_computation.26 | loop fusion | flops 3145728 | bytes 6291460 | tf_op jit(solution)/shard_map/stack | solution.py:48
  94.4 8.9 %shard_map.78 = bf16[128,1152]{1,0:T(8,128)(2,1)S(1)} custom-call(bf16[128,2304]{1,0:T(8,128)(2,1)S(1)} %copy.48.rows_ref, bf16[3,2304,2,1152]{3,2,1,0:T(2,128)(2,1)} %weight_ref.5), custom_call_target="tpu_custom_call" | custom-call | flops 2717908992 | bytes 10616832 | tf_op jit(solution)/shard_map/pallas_call | solution.py:113
  103.3 3.4 %fusion.11 = f32[128,2304]{1,0:T(8,128)S(1)} fusion(bf16[128,1152]{1,0:T(8,128)(2,1)S(1)} %shard_map.78, bf16[3,1152,2304]{2,1,0:T(8,128)(2,1)} %param.8), kind=kOutput, calls=%fused_computation.15 | convolution fusion | flops 679477248 | bytes 6782976 | tf_op jit(solution)/shard_map/dot_general | solution.py:151
  108.4 9.0 %shard_map.79 = bf16[128,1152]{1,0:T(8,128)(2,1)S(1)} custom-call(bf16[128,2304]{1,0:T(8,128)(2,1)S(1)} %copy.52.rows_ref, bf16[3,2304,2,1152]{3,2,1,0:T(2,128)(2,1)} %weight_ref.5), custom_call_target="tpu_custom_call" | custom-call | flops 2717908992 | bytes 10616832 | tf_op jit(solution)/shard_map/pallas_call | solution.py:113
  117.4 4.5 %fusion.9 = f32[128,2304]{1,0:T(8,128)} fusion(bf16[128,1152]{1,0:T(8,128)(2,1)S(1)} %shard_map.79, bf16[3,1152,2304]{2,1,0:T(8,128)(2,1)} %param.8), kind=kOutput, calls=%fused_computation.13 | convolution fusion | flops 679477248 | bytes 6782976 | tf_op jit(solution)/shard_map/dot_general | solution.py:151
  128.8 4.6 %collective-permute-done.24 = bf16[4,1,128,288]{2,3,0,1:T(8,128)(2,1)S(1)} collective-permute-done((bf16[4,1,128,288]{2,3,0,1:T(8,128)(2,1)S(1)}, bf16[4,1,128,288]{2,3,0,1:T(8,128)(2,1)S(1)}, u32[]{:S(2)}, u32[]{:S(2)}) %collective-permute-start.24) | collective-permute-done | bytes 294944 | tf_op jit(solution)/shard_map/ppermute | solution.py:64
  134.8 3.7 %collective-permute-start.26 = (bf16[1,128,288]{1,2,0:T(8,128)(2,1)}, bf16[1,128,288]{1,2,0:T(8,128)(2,1)S(1)}, u32[]{:S(2)}, u32[]{:S(2)}) collective-permute-start(bf16[1,128,288]{1,2,0:T(8,128)(2,1)} %get-tuple-element.39), channel_id=1, source_target_pairs={{0,4},{1,5},{2,6},{3,7},{4,0},{5,1},{6,2},{7,3},{8,12},{9,13},{10,... | collective-permute-start | bytes 221192 | tf_op jit(solution)/shard_map/ppermute | solution.py:72
  153.6 3.9 %select_bitcast_fusion = (bf16[2,1,3,128,2048]{4,3,2,0,1:T(8,128)(2,1)S(1)}, bf16[2,1,3,128,2048]{4,3,2,0,1:T(8,128)(2,1)S(1)}) fusion(bf16[2,3,128,2048]{3,2,1,0:T(8,128)(2,1)} %collective-permute-done.9, pred[]{:T(512)S(6)} %eq.5, s32[]{:T(128)S(6)} %select_n.168, bf16[1,3,128,2048]{3,2,1,0:T(8,128)(2,1)S(1)} %bitcast.303, ...), kind=kLoop, calls=%fused_computation.27 | loop fusion | flops 6291456 | bytes 12582917 | tf_op jit(solution)/shard_map/stack | solution.py:53
  176.8 4.2 %fusion.79 = f32[512,576]{0,1:T(8,128)} fusion(f32[512,576]{0,1:T(8,128)S(1)} %copy-done.11, f32[512,576]{0,1:T(8,128)S(1)} %fusion.49, bf16[512,2048]{1,0:T(8,128)(2,1)S(1)} %bitcast.323, bf16[6,2048,576]{1,2,0:T(8,128)(2,1)} %param.11), kind=kOutput, calls=%fused_computation.67 | convolution fusion | flops 1208549376 | bytes 7995392 | tf_op jit(solution)/shard_map/dot_general | solution.py:166
  183.6 8.2 %collective-permute-done.10 = bf16[4,2,128,288]{2,3,0,1:T(8,128)(2,1)} collective-permute-done((bf16[4,2,128,288]{2,3,0,1:T(8,128)(2,1)}, bf16[4,2,128,288]{2,3,0,1:T(8,128)(2,1)}, u32[]{:S(2)}, u32[]{:S(2)}) %collective-permute-start.10) | collective-permute-done | bytes 589856 | tf_op jit(solution)/shard_map/ppermute | solution.py:64
  201.3 4.9 %collective-permute-done.12 = bf16[2,128,288]{1,2,0:T(8,128)(2,1)S(1)} collective-permute-done((bf16[2,128,288]{1,2,0:T(8,128)(2,1)S(1)}, bf16[2,128,288]{1,2,0:T(8,128)(2,1)S(1)}, u32[]{:S(2)}, u32[]{:S(2)}) %collective-permute-start.12) | collective-permute-done | bytes 147488 | tf_op jit(solution)/shard_map/ppermute | solution.py:72
  206.2 5.1 %collective-permute-start.18 = (bf16[1,128,288]{1,2,0:T(8,128)(2,1)S(1)}, bf16[1,128,288]{1,2,0:T(8,128)(2,1)S(1)}, u32[]{:S(2)}, u32[]{:S(2)}) collective-permute-start(bf16[1,128,288]{1,2,0:T(8,128)(2,1)S(1)} %get-tuple-element.41), channel_id=1, source_target_pairs={{0,6},{1,7},{2,0},{3,1},{4,2},{5,3},{6,4},{7,5},{8,14},{9,15},{10,... | collective-permute-start | bytes 221192 | tf_op jit(solution)/shard_map/ppermute | solution.py:72
  215.5 4.4 %collective-permute-start.19 = (f32[1,128,288]{1,2,0:T(8,128)S(1)}, f32[1,128,288]{1,2,0:T(8,128)S(1)}, u32[]{:S(2)}, u32[]{:S(2)}) collective-permute-start(f32[1,128,288]{1,2,0:T(8,128)S(1)} %fusion.97), channel_id=1, source_target_pairs={{0,0},{1,1},{2,8},{3,9},{4,16},{5,17},{6,24},{7,25},{8,2},{9,3},{1... | collective-permute-start | bytes 442376 | tf_op jit(solution)/shard_map/ppermute | solution.py:176
  221.1 12.1 %collective-permute-done.14 = f32[2,128,288]{1,2,0:T(8,128)S(1)} collective-permute-done((f32[2,128,288]{1,2,0:T(8,128)S(1)}, f32[2,128,288]{1,2,0:T(8,128)S(1)}, u32[]{:S(2)}, u32[]{:S(2)}) %collective-permute-start.14) | collective-permute-done | bytes 294944 | tf_op jit(solution)/shard_map/ppermute | solution.py:176
  (143 shorter events, 87.8 us)
Async XLA Ops:
  1.6 25.9 %collective-permute-start.4 = (bf16[2,128,288]{1,2,0:T(8,128)(2,1)S(1)}, bf16[2,128,288]{1,2,0:T(8,128)(2,1)S(1)}, u32[]{:S(2)}, u32[]{:S(2)}) collective-permute-start(bf16[2,128,288]{1,2,0:T(8,128)(2,1)S(1)} %slice.101), channel_id=1, source_target_pairs={{0,6},{1,7},{2,0},{3,1},{4,2},{5,3},{6,4},{7,5},{8,14},{9,15},{10,... | collective-permute-start | bytes 442376 | tf_op jit(solution)/shard_map/ppermute | solution.py:27
  5.3 22.3 %collective-permute-start.5 = (bf16[2,128,288]{1,2,0:T(8,128)(2,1)S(1)}, bf16[2,128,288]{1,2,0:T(8,128)(2,1)S(1)}, u32[]{:S(2)}, u32[]{:S(2)}) collective-permute-start(bf16[2,128,288]{1,2,0:T(8,128)(2,1)S(1)} %slice.101), channel_id=1, source_target_pairs={{0,4},{1,5},{2,6},{3,7},{4,0},{5,1},{6,2},{7,3},{8,12},{9,13},{10,... | collective-permute-start | bytes 442376 | tf_op jit(solution)/shard_map/ppermute | solution.py:27
  5.3 22.3 %collective-permute-start.6 = (bf16[2,128,288]{1,2,0:T(8,128)(2,1)S(1)}, bf16[2,128,288]{1,2,0:T(8,128)(2,1)S(1)}, u32[]{:S(2)}, u32[]{:S(2)}) collective-permute-start(bf16[2,128,288]{1,2,0:T(8,128)(2,1)S(1)} %slice.101), channel_id=1, source_target_pairs={{0,2},{1,3},{2,4},{3,5},{4,6},{5,7},{6,0},{7,1},{8,10},{9,11},{10,... | collective-permute-start | bytes 442376 | tf_op jit(solution)/shard_map/ppermute | solution.py:27
  7.2 10.0 %collective-permute-start = (bf16[1,128,288]{1,2,0:T(8,128)(2,1)S(1)}, bf16[1,128,288]{1,2,0:T(8,128)(2,1)S(1)}, u32[]{:S(2)}, u32[]{:S(2)}) collective-permute-start(bf16[1,128,288]{1,2,0:T(8,128)(2,1)S(1)} %slice.100), channel_id=1, source_target_pairs={{0,6},{1,7},{2,0},{3,1},{4,2},{5,3},{6,4},{7,5},{8,14},{9,15},{10,... | collective-permute-start | bytes 221192 | tf_op jit(solution)/shard_map/ppermute | solution.py:27
  10.0 14.1 %collective-permute-start.1 = (bf16[1,128,288]{1,2,0:T(8,128)(2,1)S(1)}, bf16[1,128,288]{1,2,0:T(8,128)(2,1)S(1)}, u32[]{:S(2)}, u32[]{:S(2)}) collective-permute-start(bf16[1,128,288]{1,2,0:T(8,128)(2,1)S(1)} %slice.100), channel_id=1, source_target_pairs={{0,4},{1,5},{2,6},{3,7},{4,0},{5,1},{6,2},{7,3},{8,12},{9,13},{10,... | collective-permute-start | bytes 221192 | tf_op jit(solution)/shard_map/ppermute | solution.py:27
  26.0 10.0 %collective-permute-start.3 = (bf16[4,1,128,288]{2,3,0,1:T(8,128)(2,1)S(1)}, bf16[4,1,128,288]{2,3,0,1:T(8,128)(2,1)S(1)}, u32[]{:S(2)}, u32[]{:S(2)}) collective-permute-start(bf16[4,1,128,288]{2,3,0,1:T(8,128)(2,1)S(1)} %constant_dynamic-slice_fusion.1), channel_id=1, source_target_pairs={{0,1},{1,0},{2,3},{3,2},{4,5},{5,4},{6,7},{7,6},{8,9},{9,8},{10,11... | collective-permute-start | bytes 884744 | tf_op jit(solution)/shard_map/ppermute | solution.py:32
  27.8 17.5 %collective-permute-start.7 = (bf16[4,2,128,288]{2,3,0,1:T(8,128)(2,1)S(1)}, bf16[4,2,128,288]{2,3,0,1:T(8,128)(2,1)S(1)}, u32[]{:S(2)}, u32[]{:S(2)}) collective-permute-start(bf16[4,2,128,288]{2,3,0,1:T(8,128)(2,1)S(1)} %constant_dynamic-slice_fusion), channel_id=1, source_target_pairs={{0,1},{1,0},{2,3},{3,2},{4,5},{5,4},{6,7},{7,6},{8,9},{9,8},{10,11... | collective-permute-start | bytes 1769480 | tf_op jit(solution)/shard_map/ppermute | solution.py:32
  56.3 33.3 %collective-permute-start.8 = (bf16[3,128,2048]{2,1,0:T(8,128)(2,1)S(1)}, bf16[3,128,2048]{2,1,0:T(8,128)(2,1)}, u32[]{:S(2)}, u32[]{:S(2)}) collective-permute-start(bf16[3,128,2048]{2,1,0:T(8,128)(2,1)S(1)} %pad_maximum_fusion.1), channel_id=1, source_target_pairs={{0,16},{8,24},{16,0},{24,8},{1,17},{9,25},{17,1},{25,9},{2,18},{10... | collective-permute-start | bytes 4718600 | tf_op jit(solution)/shard_map/ppermute | solution.py:45
  94.4 59.3 %collective-permute-start.9 = (bf16[2,3,128,2048]{3,2,1,0:T(8,128)(2,1)}, bf16[2,3,128,2048]{3,2,1,0:T(8,128)(2,1)}, u32[]{:S(2)}, u32[]{:S(2)}) collective-permute-start(bf16[2,3,128,2048]{3,2,1,0:T(8,128)(2,1)} %fusion.19), channel_id=1, source_target_pairs={{0,8},{8,0},{16,24},{24,16},{1,9},{9,1},{17,25},{25,17},{2,10},{10... | collective-permute-start | bytes 9437192 | tf_op jit(solution)/shard_map/ppermute | solution.py:50
  123.5 9.9 %collective-permute-start.24 = (bf16[4,1,128,288]{2,3,0,1:T(8,128)(2,1)S(1)}, bf16[4,1,128,288]{2,3,0,1:T(8,128)(2,1)S(1)}, u32[]{:S(2)}, u32[]{:S(2)}) collective-permute-start(bf16[4,1,128,288]{2,3,0,1:T(8,128)(2,1)S(1)} %fusion.89), channel_id=1, source_target_pairs={{0,1},{1,0},{2,3},{3,2},{4,5},{5,4},{6,7},{7,6},{8,9},{9,8},{10,11... | collective-permute-start | bytes 884744 | tf_op jit(solution)/shard_map/ppermute | solution.py:64
  127.9 17.9 %collective-permute-start.20 = (bf16[4,2,128,288]{2,3,0,1:T(8,128)(2,1)}, bf16[4,2,128,288]{2,3,0,1:T(8,128)(2,1)}, u32[]{:S(2)}, u32[]{:S(2)}) collective-permute-start(bf16[4,2,128,288]{2,3,0,1:T(8,128)(2,1)} %fusion.87), channel_id=1, source_target_pairs={{0,1},{1,0},{2,3},{3,2},{4,5},{5,4},{6,7},{7,6},{8,9},{9,8},{10,11... | collective-permute-start | bytes 1769480 | tf_op jit(solution)/shard_map/ppermute | solution.py:64
  134.8 8.1 %collective-permute-start.26 = (bf16[1,128,288]{1,2,0:T(8,128)(2,1)}, bf16[1,128,288]{1,2,0:T(8,128)(2,1)S(1)}, u32[]{:S(2)}, u32[]{:S(2)}) collective-permute-start(bf16[1,128,288]{1,2,0:T(8,128)(2,1)} %get-tuple-element.39), channel_id=1, source_target_pairs={{0,4},{1,5},{2,6},{3,7},{4,0},{5,1},{6,2},{7,3},{8,12},{9,13},{10,... | collective-permute-start | bytes 221192 | tf_op jit(solution)/shard_map/ppermute | solution.py:72
  149.3 70.7 %collective-permute-start.21 = (bf16[2,128,288]{1,2,0:T(8,128)(2,1)}, bf16[2,128,288]{1,2,0:T(8,128)(2,1)}, u32[]{:S(2)}, u32[]{:S(2)}) collective-permute-start(bf16[2,128,288]{1,2,0:T(8,128)(2,1)} %get-tuple-element.29), channel_id=1, source_target_pairs={{0,2},{1,3},{2,4},{3,5},{4,6},{5,7},{6,0},{7,1},{8,10},{9,11},{10,... | collective-permute-start | bytes 442376 | tf_op jit(solution)/shard_map/ppermute | solution.py:72
  150.3 69.7 %collective-permute-start.22 = (bf16[2,128,288]{1,2,0:T(8,128)(2,1)}, bf16[2,128,288]{1,2,0:T(8,128)(2,1)}, u32[]{:S(2)}, u32[]{:S(2)}) collective-permute-start(bf16[2,128,288]{1,2,0:T(8,128)(2,1)} %get-tuple-element.31), channel_id=1, source_target_pairs={{0,4},{1,5},{2,6},{3,7},{4,0},{5,1},{6,2},{7,3},{8,12},{9,13},{10,... | collective-permute-start | bytes 442376 | tf_op jit(solution)/shard_map/ppermute | solution.py:72
  175.2 16.6 %collective-permute-start.10 = (bf16[4,2,128,288]{2,3,0,1:T(8,128)(2,1)}, bf16[4,2,128,288]{2,3,0,1:T(8,128)(2,1)}, u32[]{:S(2)}, u32[]{:S(2)}) collective-permute-start(bf16[4,2,128,288]{2,3,0,1:T(8,128)(2,1)} %fusion.86), channel_id=1, source_target_pairs={{0,1},{1,0},{2,3},{3,2},{4,5},{5,4},{6,7},{7,6},{8,9},{9,8},{10,11... | collective-permute-start | bytes 1769480 | tf_op jit(solution)/shard_map/ppermute | solution.py:64
  182.7 13.9 %collective-permute-start.15 = (bf16[4,1,128,288]{2,3,1,0:T(8,128)(2,1)S(1)}, bf16[4,1,128,288]{2,3,1,0:T(8,128)(2,1)S(1)}, u32[]{:S(2)}, u32[]{:S(2)}) collective-permute-start(bf16[4,1,128,288]{2,3,1,0:T(8,128)(2,1)S(1)} %fusion.88), channel_id=1, source_target_pairs={{0,1},{1,0},{2,3},{3,2},{4,5},{5,4},{6,7},{7,6},{8,9},{9,8},{10,11... | collective-permute-start | bytes 884744 | tf_op jit(solution)/shard_map/ppermute | solution.py:64
  193.1 8.2 %collective-permute-start.11 = (bf16[2,128,288]{1,2,0:T(8,128)(2,1)S(1)}, bf16[2,128,288]{1,2,0:T(8,128)(2,1)S(1)}, u32[]{:S(2)}, u32[]{:S(2)}) collective-permute-start(bf16[2,128,288]{1,2,0:T(8,128)(2,1)S(1)} %get-tuple-element.32), channel_id=1, source_target_pairs={{0,2},{1,3},{2,4},{3,5},{4,6},{5,7},{6,0},{7,1},{8,10},{9,11},{10,... | collective-permute-start | bytes 442376 | tf_op jit(solution)/shard_map/ppermute | solution.py:72
  193.7 12.5 %collective-permute-start.12 = (bf16[2,128,288]{1,2,0:T(8,128)(2,1)S(1)}, bf16[2,128,288]{1,2,0:T(8,128)(2,1)S(1)}, u32[]{:S(2)}, u32[]{:S(2)}) collective-permute-start(bf16[2,128,288]{1,2,0:T(8,128)(2,1)S(1)} %get-tuple-element.34), channel_id=1, source_target_pairs={{0,4},{1,5},{2,6},{3,7},{4,0},{5,1},{6,2},{7,3},{8,12},{9,13},{10,... | collective-permute-start | bytes 442376 | tf_op jit(solution)/shard_map/ppermute | solution.py:72
  196.6 9.6 %collective-permute-start.13 = (bf16[2,128,288]{1,2,0:T(8,128)(2,1)S(1)}, bf16[2,128,288]{1,2,0:T(8,128)(2,1)S(1)}, u32[]{:S(2)}, u32[]{:S(2)}) collective-permute-start(bf16[2,128,288]{1,2,0:T(8,128)(2,1)S(1)} %get-tuple-element.33), channel_id=1, source_target_pairs={{0,6},{1,7},{2,0},{3,1},{4,2},{5,3},{6,4},{7,5},{8,14},{9,15},{10,... | collective-permute-start | bytes 442376 | tf_op jit(solution)/shard_map/ppermute | solution.py:72
  201.3 10.1 %collective-permute-start.16 = (bf16[1,128,288]{1,2,0:T(8,128)(2,1)S(1)}, bf16[1,128,288]{1,2,0:T(8,128)(2,1)S(1)}, u32[]{:S(2)}, u32[]{:S(2)}) collective-permute-start(bf16[1,128,288]{1,2,0:T(8,128)(2,1)S(1)} %get-tuple-element.40), channel_id=1, source_target_pairs={{0,2},{1,3},{2,4},{3,5},{4,6},{5,7},{6,0},{7,1},{8,10},{9,11},{10,... | collective-permute-start | bytes 221192 | tf_op jit(solution)/shard_map/ppermute | solution.py:72
  206.2 9.2 %collective-permute-start.18 = (bf16[1,128,288]{1,2,0:T(8,128)(2,1)S(1)}, bf16[1,128,288]{1,2,0:T(8,128)(2,1)S(1)}, u32[]{:S(2)}, u32[]{:S(2)}) collective-permute-start(bf16[1,128,288]{1,2,0:T(8,128)(2,1)S(1)} %get-tuple-element.41), channel_id=1, source_target_pairs={{0,6},{1,7},{2,0},{3,1},{4,2},{5,3},{6,4},{7,5},{8,14},{9,15},{10,... | collective-permute-start | bytes 221192 | tf_op jit(solution)/shard_map/ppermute | solution.py:72
  211.4 8.5 %collective-permute-start.23 = (bf16[2,128,288]{1,2,0:T(8,128)(2,1)S(1)}, bf16[2,128,288]{1,2,0:T(8,128)(2,1)S(1)}, u32[]{:S(2)}, u32[]{:S(2)}) collective-permute-start(bf16[2,128,288]{1,2,0:T(8,128)(2,1)S(1)} %copy-done.10), channel_id=1, source_target_pairs={{0,6},{1,7},{2,0},{3,1},{4,2},{5,3},{6,4},{7,5},{8,14},{9,15},{10,... | collective-permute-start | bytes 442376 | tf_op jit(solution)/shard_map/ppermute | solution.py:72
  212.2 21.0 %collective-permute-start.14 = (f32[2,128,288]{1,2,0:T(8,128)S(1)}, f32[2,128,288]{1,2,0:T(8,128)S(1)}, u32[]{:S(2)}, u32[]{:S(2)}) collective-permute-start(f32[2,128,288]{1,2,0:T(8,128)S(1)} %fusion.93), channel_id=1, source_target_pairs={{0,0},{1,1},{2,8},{3,9},{4,16},{5,17},{6,24},{7,25},{8,2},{9,3},{1... | collective-permute-start | bytes 884744 | tf_op jit(solution)/shard_map/ppermute | solution.py:176
  215.5 20.4 %collective-permute-start.19 = (f32[1,128,288]{1,2,0:T(8,128)S(1)}, f32[1,128,288]{1,2,0:T(8,128)S(1)}, u32[]{:S(2)}, u32[]{:S(2)}) collective-permute-start(f32[1,128,288]{1,2,0:T(8,128)S(1)} %fusion.97), channel_id=1, source_target_pairs={{0,0},{1,1},{2,8},{3,9},{4,16},{5,17},{6,24},{7,25},{8,2},{9,3},{1... | collective-permute-start | bytes 442376 | tf_op jit(solution)/shard_map/ppermute | solution.py:176
  (21 other events, 158.4 us)
